TPU v7x, 32 devices: a whole 2x2x4 slice. The times are simulated.
32 devices in a mesh: dp: 8 (over y, x, core), tensor: 4 (over z).
Axes of the slice: x: 2, y: 2, z: 4, core: 2. Of those that a mesh axis runs over, the one named last changes fastest.
Arguments:
- tokens: bfloat16 [9216, 768], P('dp'), may hold values from -6 to 6
- lengths: int32 [24], P('dp'), may hold values from 32 to 1024, as said below
- gain_mix: float32 [768], replicated, may hold values from 0.5 to 1.5
- shift_mix: float32 [768], replicated, may hold values from -2.5 to 2.5
- in_weight: bfloat16 [768, 2304], replicated, may hold values from -0.21875 to 0.21875
- short_kernel: float32 [3, 2304], replicated, may hold values from -2.5 to 2.5
- skip_gain: float32 [768], replicated, may hold values from -2.5 to 2.5
- decay_rate: float32 [1536], replicated, may hold values from 0.00029296876 to 0.0390625
- filter_one: float32 [5, 128], replicated, may hold values from -6 to 6
- filter_two: float32 [128, 128], replicated, may hold values from -0.5 to 0.5
- filter_three: float32 [128, 1536], replicated, may hold values from -0.0625 to 0.0625
- out_weight: bfloat16 [768, 768], replicated, may hold values from -0.21875 to 0.21875
- gain_ffn: float32 [768], replicated, may hold values from 0.5 to 1.5
- shift_ffn: float32 [768], replicated, may hold values from -2.5 to 2.5
- gate_first: bfloat16 [4, 192, 768], P(None, None, 'tensor'), may hold values from -0.4375 to 0.4375
- gate_second: float32 [4, 4, 768], P(None, None, 'tensor'), may hold values from -3 to 3
- up_first: bfloat16 [4, 192, 768], P(None, None, 'tensor'), may hold values from -0.4375 to 0.4375
- up_second: float32 [4, 4, 768], P(None, None, 'tensor'), may hold values from -3 to 3
- down_first: bfloat16 [4, 768, 192], P(None, 'tensor'), may hold values from -0.21875 to 0.21875
- down_second: float32 [4, 4, 192], replicated, may hold values from -3 to 3
- cotangent: bfloat16 [9216, 768], P('dp'), may hold values from -6 to 6
Outputs:
- result: float32 [9216, 768], P('dp')
- grad_tokens: float32 [9216, 768], P('dp')
- grad_gain_mix: float32 [768], replicated
- grad_shift_mix: float32 [768], replicated
- grad_in_weight: float32 [768, 2304], replicated
- grad_short_kernel: float32 [3, 2304], replicated
- grad_skip_gain: float32 [768], replicated
- grad_decay_rate: float32 [1536], replicated
- grad_filter_one: float32 [5, 128], replicated
- grad_filter_two: float32 [128, 128], replicated
- grad_filter_three: float32 [128, 1536], replicated
- grad_out_weight: float32 [768, 768], replicated
- grad_gain_ffn: float32 [768], replicated
- grad_shift_ffn: float32 [768], replicated
- grad_gate_first: float32 [4, 192, 768], P(None, None, 'tensor')
- grad_gate_second: float32 [4, 4, 768], P(None, None, 'tensor')
- grad_up_first: float32 [4, 192, 768], P(None, None, 'tensor')
- grad_up_second: float32 [4, 4, 768], P(None, None, 'tensor')
- grad_down_first: float32 [4, 768, 192], P(None, 'tensor')
- grad_down_second: float32 [4, 4, 192], replicated
Inputs may be any that keep to these rules, and one draw needn't show every extreme that they name: `lengths`: each device holds 3 sequences, one per bucket row, each filling the first positions of its row: the first in the long row with more than half of 1024 tokens, the others in short rows with at least half of 64 tokens.
All inputs are finite; a program needn't handle non-finite values.
Results may differ from a plain program's by a relative error of at most 0.0096.
Values sent between devices are 32-bit elements; how exact they have to be, the bound alone decides.
A program may use at most 320 MiB of HBM per device.

v0:
```python
import functools
import math

import jax
import jax.numpy as jnp
import numpy as np
from jax import lax
from jax.experimental import pallas as pl
from jax.experimental.pallas import tpu as pltpu
from jax.sharding import PartitionSpec as P

LONG = 1024
SHORT = 64
TOK = LONG + 2 * SHORT
D = 768
NB = 4
DB = 192
LEAF = 256
CT = 256
ORDER = 128
EPSILON = 1e-05
PRECISE = lax.Precision.HIGHEST
F32 = jnp.float32
BF16 = jnp.bfloat16
MESH = pl.DeviceIdType.MESH
ROOT = math.sqrt(0.5)
MIB = 1 << 20

WBASE = (0, 128, 384, 512)
WSKIP = (0, 64, 0, 64)

PADDED = ((0, LONG, 8), (LONG, SHORT, LONG + 16), (LONG + SHORT, SHORT, LONG + SHORT + 24))
PADROWS = TOK + 32
CHUNK = 64
CHUNKS = TOK // CHUNK
HALVES = (slice(0, 128), slice(128, 256))


def transforms():
    step = np.arange(256)
    angle = 2.0 * np.pi * np.outer(step, np.arange(512)) / 512
    real, imag = np.cos(angle), -np.sin(angle)
    imag[0] = np.cos(np.pi * np.arange(512))
    forward = [np.concatenate([real, imag], 0)]
    for turn in (np.pi / 2, np.pi / 4, np.pi / 4 + np.pi):
        angle = np.outer((turn + 2.0 * np.pi * step) / 256, np.arange(256))
        cos, sin = np.cos(angle), np.sin(angle)
        forward.append(np.block([[cos, -sin], [sin, cos]]))
    weight = np.full(512, 2.0)
    weight[[0, 256]] = 1.0
    back = [forward[0].T * weight[None, :] / 512]
    back += [table.T / 256 for table in forward[1:]]
    step = np.arange(64)
    angle = 2.0 * np.pi * np.outer(step, np.arange(128)) / 128
    real, imag = np.cos(angle), -np.sin(angle)
    imag[0] = np.cos(np.pi * np.arange(128))
    short = np.concatenate([real, imag], 0)
    weight = np.full(128, 2.0)
    weight[[0, 64]] = 1.0
    short_back = short.T * weight[None, :] / 128
    return tuple(
        np.asarray(table, np.float32).astype(BF16)
        for table in (np.stack(forward), np.stack(back), short, short_back)
    )


def filter_places():
    return np.concatenate([np.arange(LONG), LONG - np.arange(LONG)]).astype(np.float32)


def filter_features():
    places = filter_places().astype(np.float64)
    turning = places * (2.0 * math.pi / LONG)
    return np.stack(
        [places / LONG, np.cos(turning), np.sin(turning), np.cos(2 * turning), np.sin(2 * turning)], 1
    ).astype(np.float32)


GAIN, SHIFT, SKIP, RATE, GAIN_TWO, SHIFT_TWO = 0, 1, 2, 3, 5, 6

ROWS_AT = (0, NB * DB, 2 * NB * DB, 3 * NB * DB, 3 * NB * DB + 3 * NB * NB)
REST_START = 3 * NB * DB + 64
REST_AT = (REST_START, REST_START + NB * DB, REST_START + NB * DB + 2 * DB)
PACKED = REST_AT[2] + 2 * NB * NB

LOCAL = 8

MISC_TAPS = 4 * ORDER
MISC_SKIP = MISC_TAPS + 32
MISC_RATE = MISC_SKIP + 2
MISC_TWO = MISC_SKIP + 8
MISC_ONE = MISC_TWO + ORDER
MISC_GLU = MISC_ONE + 8
MISC_ROWS = MISC_GLU + 48


def lane_cuts(rows, lanes, middle):
    return ((slice(0, rows), slice(0, middle)), (slice(0, rows), slice(middle, lanes)))


def early_cuts(rows, lanes):
    middle = up_to(rows // 2, 8)
    return ((slice(0, middle), slice(0, lanes)), (slice(middle, rows), slice(0, lanes)))


def sin_cos(angle):
    turns = jnp.floor(angle * (2.0 / math.pi) + 0.5)
    rest = ((angle - turns * 1.5703125) - turns * 4.837512969970703e-4) - turns * 7.54978995489188e-8
    square = rest * rest
    sine = rest + rest * square * (-1.6666654611e-1 + square * (8.3321608736e-3 - square * 1.9515295891e-4))
    cosine = square * square * (4.166664568298827e-2 + square * (-1.388731625493765e-3 + square * 2.443315711809948e-5))
    cosine = cosine + (1.0 - 0.5 * square)
    quarter = turns - 4.0 * jnp.floor(turns * 0.25)
    odd = (quarter == 1.0) | (quarter == 3.0)
    first, second = jnp.where(odd, cosine, sine), jnp.where(odd, sine, cosine)
    return (
        jnp.where(quarter >= 2.0, -first, first),
        jnp.where((quarter == 1.0) | (quarter == 2.0), -second, second),
    )


def rows_of(place, size):
    return pl.ds(pl.multiple_of(place, size), size)


def padded_place(chunk):
    return pl.multiple_of(8 + chunk * CHUNK + 8 * jnp.maximum(chunk - (LONG // CHUNK - 1), 0), 8)


def mask_of(valid, rows):
    half = valid[rows, :]
    return jnp.concatenate([half, half], axis=1)


def dot(a, b):
    return jnp.dot(a, b, preferred_element_type=F32)


def dot_nt(a, b):
    return lax.dot_general(a, b, (((1,), (1,)), ((), ())), preferred_element_type=F32)


def dot_tn(a, b):
    return lax.dot_general(a, b, (((0,), (0,)), ((), ())), preferred_element_type=F32)


def zero_pads(buffer):
    for place in (0, 8 + LONG, 16 + LONG + SHORT, 24 + LONG + 2 * SHORT):
        buffer[:, place : place + 8, :] = jnp.zeros((buffer.shape[0], 8, buffer.shape[2]), F32)


def conv_taps(buffer, part, place, taps, lanes):
    slab = buffer[part, pl.ds(pl.multiple_of(place - 8, 8), CHUNK + 8), lanes]
    now, one, two = slab[8:], pltpu.roll(slab, 1, 0)[8:], pltpu.roll(slab, 2, 0)[8:]
    return taps[0:1, lanes] * now + taps[1:2, lanes] * one + taps[2:3, lanes] * two


def half_lanes(index):
    step = lax.div(index, 2)
    return step * 16, pl.ds(pl.multiple_of((index - 2 * step) * 128, 128), 128)


def fold_rows(signal, leaves, signed=None):
    def step(index, carry):
        place, lanes = half_lanes(index)
        low = [signal[rows_of(place + LEAF * part, 16), lanes] for part in range(4)]
        even = odd = low
        if signed is not None:
            high = [signed[rows_of(place + LEAF * part, 16), lanes] for part in range(4)]
            even = [a + b for a, b in zip(low, high)]
            odd = [a - b for a, b in zip(low, high)]
        first, second = rows_of(place, 16), rows_of(place + LEAF, 16)
        leaves[0, first, lanes] = (even[0] + even[2]).astype(BF16)
        leaves[0, second, lanes] = (even[1] + even[3]).astype(BF16)
        leaves[1, first, lanes] = (even[0] - even[2]).astype(BF16)
        leaves[1, second, lanes] = (even[1] - even[3]).astype(BF16)
        turned = (odd[1] - odd[3]) * ROOT
        other = (odd[1] + odd[3]) * ROOT
        leaves[2, first, lanes] = (odd[0] + turned).astype(BF16)
        leaves[2, second, lanes] = (odd[2] + other).astype(BF16)
        leaves[3, first, lanes] = (odd[0] - turned).astype(BF16)
        leaves[3, second, lanes] = (odd[2] - other).astype(BF16)
        return carry

    lax.fori_loop(0, 2 * LEAF // 16, step, 0, unroll=4)


def unfold_rows(parts, place, lanes):
    first, second = rows_of(place, 16), rows_of(place + LEAF, 16)
    a, b = parts[0, first, lanes], parts[0, second, lanes]
    c, d = parts[1, first, lanes], parts[1, second, lanes]
    e, f = parts[2, first, lanes], parts[2, second, lanes]
    g, h = parts[3, first, lanes], parts[3, second, lanes]
    cyclic = (a + c, b + d, a - c, b - d)
    turned, other = (e - g) * ROOT, (f - h) * ROOT
    negative = (e + g, turned + other, f + h, other - turned)
    return cyclic, negative


def transform(table, leaves, out):
    def step(leaf, carry):
        out[leaf] = dot(table[leaf], leaves[leaf]).astype(out.dtype)
        return carry

    lax.fori_loop(0, 4, step, 0)


def product(left, right, out, conjugate):
    steps = LEAF // 16

    def step(index, carry):
        leaf = lax.div(index, steps)
        place = (index - leaf * steps) * 16
        real, imag = rows_of(place, 16), rows_of(place + LEAF, 16)
        a, b = left[leaf, real, :].astype(F32), left[leaf, imag, :].astype(F32)
        c, d = right[leaf, real, :].astype(F32), right[leaf, imag, :].astype(F32)
        ac, bd = a * c, b * d
        if conjugate:
            new_real, new_imag = ac + bd, b * c - a * d
        else:
            new_real, new_imag = ac - bd, a * d + b * c
        edge = (lax.broadcasted_iota(jnp.int32, a.shape, 0) + index * 16) == 0
        out[leaf, real, :] = jnp.where(edge, ac, new_real).astype(BF16)
        out[leaf, imag, :] = jnp.where(edge, bd, new_imag).astype(BF16)
        return carry

    lax.fori_loop(0, 4 * steps, step, 0, unroll=4)


def product_short(left, right, conjugate):
    a, b = left[:SHORT], left[SHORT:]
    c, d = right[:SHORT], right[SHORT:]
    ac, bd = a * c, b * d
    if conjugate:
        real, imag = ac + bd, b * c - a * d
    else:
        real, imag = ac - bd, a * d + b * c
    edge = lax.broadcasted_iota(jnp.int32, a.shape, 0) == 0
    real, imag = jnp.where(edge, ac, real), jnp.where(edge, bd, imag)
    return jnp.concatenate([real, imag], axis=0).astype(BF16)


def window_rows(side, place, rate):
    spot = lax.broadcasted_iota(jnp.int32, (16, rate.shape[1]), 0) + place
    if side == 0:
        distance = spot.astype(F32)
        return jnp.exp(-distance * rate), distance
    distance = (LONG - spot).astype(F32)
    return jnp.where(spot == 0, 0.0, jnp.exp(-distance * rate)), distance


def mixer_forward_kernel(
    ranks,
    quarters,
    lengths,
    singles,
    filters,
    weights,
    tokens,
    in_q,
    in_k,
    in_v,
    taps_q,
    taps_k,
    taps_v,
    three_f,
    three_r,
    table,
    table_back,
    short,
    short_back,
    features,
    mixed,
    total_out,
    masked_q,
    masked_k,
    masked_v,
    kernel_spec,
    source_spec,
    kernel_short,
    source_short,
    normed,
    gathered,
    valid,
    vectors,
    hidden_one,
    hidden_two,
    cos_one,
    cos_two,
    mixed_own,
    normed_own,
    padded,
    query,
    source,
    base,
    leaves,
    spec,
    parts,
    flat,
    filling,
    *sems,
):
    tile = pl.program_id(0)
    places = Places(ranks, quarters)
    rows = flat.shape[0] // ranks
    exchange = Exchange(
        places,
        early_cuts(rows, 128),
        filling if ranks <= LOCAL else gathered,
        sems,
        own=flat.at[pl.ds(pl.multiple_of(places.rank * rows, 8), rows)],
        relay=True,
        flush=gathered if ranks <= LOCAL else None,
    )
    phases = 5
    levels = exchange.levels()

    due = [[] for _ in range(phases * (D // CT))]
    for level, events in enumerate(levels):
        due[min(2 * level, len(due) - 1)] += events

    def tick(phase):
        for step in range(D // CT):
            if due[step * phases + phase]:

                @pl.when(tile == step)
                def _(step=step):
                    for event in due[step * phases + phase]:
                        event()

    @pl.when(tile == 0)
    def _():
        gate, up, down, gate_second, up_second = weights
        for block in range(NB):
            start = block * DB
            pairs = (gate[block].astype(F32), up[block].astype(F32))
            for which, value in enumerate(pairs):
                flat[ROWS_AT[which] + start : ROWS_AT[which] + start + DB, :] = value[:, 0:128]
            flat[REST_AT[0] + start : REST_AT[0] + start + DB, :] = jnp.concatenate(
                [value[:, 128:] for value in pairs], axis=1
            )
            flat[ROWS_AT[2] + start : ROWS_AT[2] + start + DB, :] = down[block].astype(F32)[:, 0:128]
            for which, value in enumerate((gate_second, up_second)):
                at = ROWS_AT[3] + which * NB * NB + block * NB
                flat[at : at + NB, :] = value[block, :, 0:128]
            at = REST_AT[2] + block * NB
            flat[at : at + NB, :] = jnp.concatenate(
                [value[block][:, 128:] for value in (gate_second, up_second)], axis=1
            )
        for block in range(2):
            start = REST_AT[1] + block * DB
            flat[start : start + DB, :] = jnp.concatenate(
                [down[side].astype(F32)[:, 128:] for side in (block, block + 2)], axis=1
            )
        greet(places, False)
        exchange.start()

        gain, shift, skip, rate, gain_two, shift_two = singles
        for row, value in enumerate((gain, shift, skip)):
            vectors[row, :] = value[...]
        vectors[RATE, :] = rate[0:D]
        vectors[RATE + 1, :] = rate[D : 2 * D]
        vectors[GAIN_TWO, :] = gain_two[...]
        vectors[SHIFT_TWO, :] = shift_two[...]
        vectors[SHIFT_TWO + 1, :] = jnp.zeros((D,), F32)
        for row, (first, count, _) in enumerate(PADDED):
            spot = lax.broadcasted_iota(jnp.int32, (count, 128), 0)
            valid[first : first + count, :] = jnp.where(spot < lengths[row], 1.0, 0.0)

        one, two = filters

        def first_layer(index, carry):
            rows = rows_of(index * 64, 64)
            angle = None
            for column in range(one.shape[0]):
                term = features[rows, column : column + 1] * one[column : column + 1, :]
                angle = term if angle is None else angle + term
            hidden_one[rows, :], cos_one[rows, :] = sin_cos(angle)
            return carry

        lax.fori_loop(0, 2 * LONG // 64, first_layer, 0, unroll=2)
        cos_two[...] = jnp.dot(hidden_one[...], two[...], precision=PRECISE, preferred_element_type=F32)

        def second_layer(index, carry):
            rows = rows_of(index * 64, 64)
            sine, cos_two[rows, :] = sin_cos(cos_two[rows, :])
            high = sine.astype(BF16)
            hidden_two[rows, 0:ORDER] = high
            hidden_two[rows, ORDER : 2 * ORDER] = (sine - high.astype(F32)).astype(BF16)
            hidden_two[rows, 2 * ORDER :] = high
            return carry

        lax.fori_loop(0, 2 * LONG // 64, second_layer, 0, unroll=2)

        def step(index, carry):
            rows = rows_of(index * 32, 32)
            x = tokens[rows, :].astype(F32)
            centre = x - jnp.mean(x, axis=1, keepdims=True)
            spread = jnp.mean(centre * centre, axis=1, keepdims=True)
            out = centre * lax.rsqrt(spread + EPSILON) * vectors[GAIN : GAIN + 1, :] + vectors[SHIFT : SHIFT + 1, :]
            normed[rows, :] = out.astype(BF16)
            return carry

        lax.fori_loop(0, TOK // 32, step, 0, unroll=4)
        for q in range(quarters):

            @pl.when(lax.axis_index("tensor") == q)
            def _(q=q):
                normed_own[...] = normed[:, q * D // quarters : (q + 1) * D // quarters]

        zero_pads(padded)

    columns = vectors[:, pl.ds(pl.multiple_of(tile * CT, CT), CT)]
    skip, rate_f, rate_r = columns[SKIP : SKIP + 1], columns[RATE : RATE + 1], columns[RATE + 1 : RATE + 2]

    for side, three in enumerate((three_f, three_r)):
        high = three[...].astype(BF16)
        low = (three[...] - high.astype(F32)).astype(BF16)
        base[side] = dot(
            hidden_two[side * LONG : (side + 1) * LONG, :], jnp.concatenate([high, high, low], axis=0)
        )

    def window_step(index, carry):
        rows = rows_of(index * 16, 16)
        for side, rate in ((0, rate_f), (1, rate_r)):
            window, _ = window_rows(side, index * 16, rate)
            base[side, rows, :] = base[side, rows, :] * window
        return carry

    lax.fori_loop(0, LONG // 16, window_step, 0, unroll=2)
    fold_rows(base.at[0], leaves, base.at[1])
    transform(table, leaves, spec)
    kernel_spec[...] = spec[...].astype(BF16)
    low = base[0, 0:SHORT, :]
    high = base[1, LONG - SHORT : LONG, :]
    high = jnp.where(lax.broadcasted_iota(jnp.int32, high.shape, 0) == 0, 0.0, high)
    narrow = dot(short[...], jnp.concatenate([low, high], axis=0).astype(BF16))
    kernel_short[...] = narrow

    tick(0)

    for part, (weight, save) in enumerate(((in_q, masked_q), (in_k, masked_k), (in_v, masked_v))):
        for start in range(0, LONG, 512):
            out = dot(normed[start : start + 512, :], weight[...]) * mask_of(valid, slice(start, start + 512))
            padded[part, 8 + start : 8 + start + 512, :] = out
            save[start : start + 512, :] = out.astype(BF16)
        out = dot(normed[LONG:, :], weight[...]) * mask_of(valid, slice(LONG, TOK))
        padded[part, LONG + 16 : LONG + 16 + SHORT, :] = out[:SHORT]
        padded[part, LONG + SHORT + 24 : LONG + 2 * SHORT + 24, :] = out[SHORT:]
        save[LONG:, :] = out.astype(BF16)

    tick(1)

    def conv_step(chunk, carry):
        place = padded_place(chunk)
        rows = rows_of(chunk * CHUNK, CHUNK)
        mask = valid[rows, :]
        for lanes in HALVES:
            query[rows, lanes] = conv_taps(padded, 0, place, taps_q, lanes) * mask
            key = conv_taps(padded, 1, place, taps_k, lanes) * mask
            source[rows, lanes] = key * conv_taps(padded, 2, place, taps_v, lanes)
        return carry

    lax.fori_loop(0, CHUNKS, conv_step, 0)

    tick(2)

    fold_rows(source, leaves)
    transform(table, leaves, source_spec)
    tick(3)
    product(source_spec, spec, leaves, False)
    transform(table_back, leaves, parts)

    def finish(rows, lanes, skip_lanes, spread):
        held = source[rows, lanes]
        total = spread + skip_lanes * held
        total_out[rows, lanes] = total.astype(BF16)
        mixed[rows, lanes] = (query[rows, lanes] * total).astype(BF16)

    for lanes in HALVES:

        def unfold_step(index, carry, lanes=lanes):
            cyclic, negative = unfold_rows(parts, index * 16, lanes)
            for part in range(4):
                rows = rows_of(index * 16 + LEAF * part, 16)
                finish(rows, lanes, skip[:, lanes], (cyclic[part] + negative[part]) * 0.25)
            return carry

        lax.fori_loop(0, LEAF // 16, unfold_step, 0, unroll=2)

    for row in range(2):
        rows = slice(LONG + SHORT * row, LONG + SHORT * (row + 1))
        spectrum = dot(short[:, 0:SHORT], source[rows, :].astype(BF16))
        source_short[row] = spectrum
        joined = product_short(spectrum, narrow, False)
        finish(rows, slice(0, CT), skip, dot(short_back[0:SHORT, :], joined))
    width = D // quarters
    for q in range(quarters):
        for part in range(D // CT):
            low, high = max(q * width, part * CT), min((q + 1) * width, (part + 1) * CT)
            if low < high:

                @pl.when((lax.axis_index("tensor") == q) & (tile == part))
                def _(q=q, part=part, low=low, high=high):
                    mixed_own[:, low - q * width : high - q * width] = mixed[:, low - part * CT : high - part * CT]

    tick(4)


def mixer_backward_kernel(
    ranks,
    quarters,
    early,
    grad_out,
    tokens,
    valid,
    vectors,
    hidden_two,
    in_q,
    in_k,
    in_v,
    taps_q,
    taps_k,
    taps_v,
    three_f,
    three_r,
    table,
    table_back,
    short,
    short_back,
    total_in,
    masked_q,
    masked_k,
    masked_v,
    kernel_spec,
    source_spec,
    kernel_short,
    source_short,
    grad_mixed,
    normed_own,
    grad_hidden,
    hidden_one,
    cos_one,
    cos_two,
    filter_two,
    features,
    grad_tokens,
    early_whole,
    out_whole,
    tile_whole,
    other_whole,
    norm_whole,
    misc_whole,
    padded,
    grad_conv,
    grad_total,
    key_value,
    leaves,
    parts,
    grad_project,
    normed_sum,
    grad_deep,
    misc,
    tile_held,
    tile_landed,
    tile_filling,
    early_held,
    early_landed,
    early_filling,
    other_held,
    other_landed,
    other_filling,
    spec_kept,
    narrow_kept,
    rate_sums,
    norm_parts,
    misc_parts,
    misc_sum,
    misc_filling,
    load_sems,
    late_sems,
    norm_sems,
    misc_sems,
    *sems,
):
    last = D // CT - 1
    tiles = last + 1
    step = pl.program_id(0)
    tile = lax.rem(step, tiles)
    columns = vectors[:, pl.ds(pl.multiple_of(tile * CT, CT), CT)]
    skip, rate_f, rate_r = columns[SKIP : SKIP + 1], columns[RATE : RATE + 1], columns[RATE + 1 : RATE + 2]
    gain = vectors[GAIN : GAIN + 1, :]
    own, quarter_rows = normed_own.shape[1], ranks * tile_held.shape[2]
    places = Places(ranks, quarters)
    rank, quarter = places.rank, places.quarter
    early_exchange = Exchange(
        places,
        early_cuts(early_held.shape[1], 128),
        early_filling if ranks <= LOCAL else early_whole,
        sems[0:5],
        held=early_held,
        landed=early_landed,
        line=False,
        flush=early_whole if ranks <= LOCAL else None,
    )
    other_exchange = Exchange(
        places,
        lane_cuts(other_held.shape[1], 256, 128),
        other_filling if ranks <= LOCAL else other_whole,
        sems[5:10],
        held=other_held,
        landed=other_landed,
        flush=other_whole if ranks <= LOCAL else None,
    )

    out_exchange = Exchange(
        places,
        lane_cuts(tile_held.shape[2], D, D // 2),
        tile_filling.at[0] if ranks <= LOCAL else out_whole,
        sems[10:15],
        held=tile_held.at[0],
        landed=tile_landed.at[0],
        flush=out_whole if ranks <= LOCAL else None,
    )

    def tile_exchange(job, buffers):
        lanes = tile_held.shape[3]
        return Exchange(
            places,
            lane_cuts(tile_held.shape[2], lanes, lanes // 2),
            tile_filling.at[buffers] if ranks <= LOCAL else tile_whole.at[job],
            [sem.at[job] for sem in sems[15:20]],
            held=tile_held.at[buffers],
            landed=tile_landed.at[buffers],
            flush=tile_whole.at[job] if ranks <= LOCAL else None,
        )

    def first_loads():
        copies = []
        for exchange, source in ((early_exchange, early), (out_exchange, grad_out)):
            height = exchange.own.shape[0]
            for stream, (rows, lanes) in enumerate(exchange.cuts):
                for slot in range(ranks):
                    start = pl.multiple_of(exchange.slot_rank(stream, slot) * height + rows.start, 8)
                    copies.append(
                        pltpu.make_async_copy(
                            source.at[pl.ds(start, rows.stop - rows.start), lanes],
                            exchange.held.at[slot, rows, lanes],
                            load_sems.at[len(copies)],
                        )
                    )
        return copies

    def late_loads():
        copies = []
        for index, source in enumerate((hidden_one, cos_one, cos_two)):
            for side in range(2):
                copies.append(
                    (
                        source.at[side * LONG : (side + 1) * LONG],
                        padded.at[index, 0:LONG, side * ORDER : (side + 1) * ORDER],
                    )
                )
        for part in range(3):
            copies.append((grad_hidden.at[:, part * CT : (part + 1) * CT], grad_conv.at[part, 0:TOK]))
        return [
            pltpu.make_async_copy(source, target, late_sems.at[index])
            for index, (source, target) in enumerate(copies)
        ]

    def token_load():
        return pltpu.make_async_copy(tokens, grad_project, late_sems.at[10])

    def norm_copy(mask):
        return pltpu.make_async_remote_copy(
            src_ref=norm_parts.at[rank],
            dst_ref=norm_parts.at[rank],
            send_sem=norm_sems.at[0, mask - 1],
            recv_sem=norm_sems.at[1, mask - 1],
            device_id={"dp": places.across[mask]},
            device_id_type=MESH,
        )

    part_rows = misc_sum.shape[0]

    def misc_copy(step, mask):
        peer = places.across[mask]
        return pltpu.make_async_remote_copy(
            src_ref=misc.at[last, pl.ds(pl.multiple_of(peer * part_rows, 8), part_rows)] if step == 0 else misc_sum,
            dst_ref=(misc_parts if step == 0 else misc_filling).at[rank],
            send_sem=misc_sems.at[step, 0, mask - 1],
            recv_sem=misc_sems.at[step, 1, mask - 1],
            device_id={"dp": peer},
            device_id_type=MESH,
        )

    def misc_start():
        misc_parts[rank] = misc[last, pl.ds(pl.multiple_of(rank * part_rows, 8), part_rows), :]
        for mask in range(1, ranks):
            misc_copy(0, mask).start()

    def misc_turn():
        for mask in range(1, ranks):
            misc_copy(0, mask).wait_recv()
        total = misc_parts[0]
        for index in range(1, ranks):
            total += misc_parts[index]
        misc_sum[...] = total
        misc_filling[rank] = total
        for mask in range(1, ranks):
            misc_copy(1, mask).start()

    def misc_finish():
        for mask in range(1, ranks):
            misc_copy(1, mask).wait_recv()
        misc_whole[...] = misc_filling[...]
        for mask in range(1, ranks):
            misc_copy(0, mask).wait_send()
            misc_copy(1, mask).wait_send()

    front, back = 9, 9
    total = tiles * (front + back)
    due = [[] for _ in range(total)]
    late = []

    def plan(levels, start, pace, stop):
        for level, events in enumerate(levels):
            if stop is None and start + pace * level >= total:
                late.append(events)
            else:
                due[min(start + pace * level, (total if stop is None else stop) - 1)] += events

    plan(early_exchange.levels(), 3, 4, total)
    plan(out_exchange.levels(), 2, 3, tiles * front - 1)
    for job in range(tiles):
        plan(tile_exchange(job, (job + 1) % 3).levels(), (job + 1) * front + 1, 3 if job < last else 2, total)
    plan(other_exchange.levels(), total - back + 4, 1, None)

    def tick(base, phase, width):
        for index in range(tiles):
            if due[base + index * width + phase]:

                @pl.when(tile == index)
                def _(index=index):
                    for event in due[base + index * width + phase]:
                        event()

    @pl.when(step == 0)
    def _():
        zero_pads(padded)
        zero_pads(grad_conv)
        tile_held[...] = jnp.zeros(tile_held.shape, F32)
        misc[...] = jnp.zeros(misc.shape, F32)
        for copy in first_loads():
            copy.start()
        norm_parts[...] = jnp.zeros(norm_parts.shape, F32)
        greet(places, True)
        for copy in first_loads():
            copy.wait()
        early_exchange.start()
        out_exchange.start()

    @pl.when(step < tiles)
    def _():
        for part, saved in enumerate((masked_q, masked_k, masked_v)):
            for start, count, place in PADDED:
                padded[part, place : place + count, :] = saved[start : start + count, :].astype(F32)

        tick(0, 0, front)
        for half, lanes in enumerate(HALVES):

            def first_step(chunk, carry, lanes=lanes):
                place = padded_place(chunk)
                rows = rows_of(chunk * CHUNK, CHUNK)
                mask = valid[rows, :]
                query = conv_taps(padded, 0, place, taps_q, lanes)
                key = conv_taps(padded, 1, place, taps_k, lanes) * mask
                value = conv_taps(padded, 2, place, taps_v, lanes) * mask
                key_value[0, rows, lanes] = key.astype(BF16)
                key_value[1, rows, lanes] = value.astype(BF16)
                incoming = grad_mixed[rows, lanes].astype(F32) * mask
                out = incoming * query
                grad_total[rows, lanes] = out
                grad_conv[0, pl.ds(place, CHUNK), lanes] = incoming * total_in[rows, lanes].astype(F32)
                return carry + (out * key * value).reshape(CHUNK // 8, 8, 128).sum(0)

            skip_sum = lax.fori_loop(0, CHUNKS, first_step, jnp.zeros((8, 128), F32), unroll=2)
            misc[tile, MISC_SKIP + half : MISC_SKIP + half + 1, :] = jnp.sum(skip_sum, axis=0, keepdims=True)
            tick(0, 1 + half, front)

        fold_rows(grad_total, leaves)
        transform(table, leaves, spec_kept.at[tile])
        tick(0, 3, front)
        product(spec_kept.at[tile], kernel_spec, leaves, True)
        transform(table_back, leaves, parts)
        tick(0, 4, front)

        def finish(rows, place, count, lanes, skip_lanes, back):
            out = back + skip_lanes * grad_total[rows, lanes]
            grad_conv[1, pl.ds(place, count), lanes] = out * key_value[1, rows, lanes].astype(F32)
            grad_conv[2, pl.ds(place, count), lanes] = out * key_value[0, rows, lanes].astype(F32)

        for lanes in HALVES:

            def unfold_step(index, carry, lanes=lanes):
                cyclic, negative = unfold_rows(parts, index * 16, lanes)
                for part in range(4):
                    rows = rows_of(index * 16 + LEAF * part, 16)
                    place = pl.multiple_of(index * 16 + LEAF * part + 8, 8)
                    finish(rows, place, 16, lanes, skip[:, lanes], (cyclic[part] + negative[part]) * 0.25)
                return carry

            lax.fori_loop(0, LEAF // 16, unfold_step, 0, unroll=2)

        narrow = jnp.zeros((2 * SHORT, CT), F32)
        for row, (start, count, place) in enumerate(PADDED[1:]):
            rows = slice(start, start + count)
            spectrum = dot(short[:, 0:SHORT], grad_total[rows, :].astype(BF16))
            joined = product_short(spectrum, kernel_short[...], True)
            finish(rows, place, count, slice(0, CT), skip, dot(short_back[0:SHORT, :], joined))
            narrow += dot(short_back[...], product_short(spectrum, source_short[row], True))
        narrow_kept[tile] = narrow
        tick(0, 5, front)

        for half, lanes in enumerate(HALVES):

            def second_step(chunk, carry, half=half, lanes=lanes):
                place = padded_place(chunk)
                rows = rows_of(chunk * CHUNK, CHUNK)
                mask = valid[rows, :]
                sums = []
                for part, taps in enumerate((taps_q, taps_k, taps_v)):
                    slab = grad_conv[part, pl.ds(place, CHUNK + 8), lanes]
                    now = slab[:CHUNK]
                    one = pltpu.roll(slab, CHUNK + 7, 0)[:CHUNK]
                    two = pltpu.roll(slab, CHUNK + 6, 0)[:CHUNK]
                    held = padded[part, pl.ds(place, CHUNK), lanes]
                    out = (taps[0:1, lanes] * now + taps[1:2, lanes] * one + taps[2:3, lanes] * two) * mask
                    at = part * CT + half * 128
                    grad_project[rows, at : at + 128] = out.astype(BF16)
                    sums += [(held * each).reshape(CHUNK // 8, 8, 128).sum(0) for each in (now, one, two)]
                return tuple(a + b for a, b in zip(carry, sums))

            sums = lax.fori_loop(0, CHUNKS, second_step, tuple(jnp.zeros((8, 128), F32) for _ in range(9)))
            for index, each in enumerate(sums):
                row = MISC_TAPS + 16 * half + index
                misc[tile, row : row + 1, :] = jnp.sum(each, axis=0, keepdims=True)
            tick(0, 6 + half, front)

        @pl.when(tile == last)
        def _():
            for copy in late_loads():
                copy.start()

        chunk = tile_held.shape[2]
        buffers = lax.rem(tile + 1, 3)
        now = tile_exchange(tile, buffers)
        outs = [dot_tn(normed_own[...], grad_project[:, part * CT : (part + 1) * CT]) for part in range(3)]
        for stream, (_, lanes) in enumerate(now.cuts):
            for source in range(ranks):
                slot = now.rank_slot(stream, source)
                if source < own // chunk:
                    for part in range(3):
                        low, high = max(lanes.start, part * CT), min(lanes.stop, (part + 1) * CT)
                        if low < high:
                            tile_held[buffers, slot, :, low:high] = outs[part][
                                source * chunk : (source + 1) * chunk, low - part * CT : high - part * CT
                            ]
        now.start()

        def project_step(index, carry):
            rows = rows_of(index * 192, 192)
            out = dot_nt(grad_project[rows, 0:CT], in_q[...])
            out += dot_nt(grad_project[rows, CT : 2 * CT], in_k[...])
            out += dot_nt(grad_project[rows, 2 * CT :], in_v[...])

            @pl.when(tile == 0)
            def _():
                normed_sum[rows, :] = out

            @pl.when(tile > 0)
            def _():
                normed_sum[rows, :] += out

            return carry

        lax.fori_loop(0, TOK // 192, project_step, 0)
        @pl.when(tile == last)
        def _():
            token_load().start()

        tick(0, 8, front)


    @pl.when(step >= tiles)
    def _():
        base = tiles * front

        @pl.when(step == tiles)
        def _():
            for copy in late_loads():
                copy.wait()
            token_load().wait()

            def norm_step(index, carry):
                rows = rows_of(index * 32, 32)
                x = grad_project[rows, :].astype(F32)
                centre = x - jnp.mean(x, axis=1, keepdims=True)
                spread = jnp.mean(centre * centre, axis=1, keepdims=True)
                scale = lax.rsqrt(spread + EPSILON)
                unit = centre * scale
                grad = normed_sum[rows, :]
                wide = grad * gain
                mean = jnp.mean(wide, axis=1, keepdims=True)
                along = jnp.mean(wide * unit, axis=1, keepdims=True)
                straight = jnp.concatenate([grad_conv[part, rows, :] for part in range(3)], axis=1)
                normed_sum[rows, :] = straight + scale * (wide - mean - unit * along)
                return (
                    carry[0] + (grad * unit).reshape(4, 8, D).sum(0),
                    carry[1] + grad.reshape(4, 8, D).sum(0),
                )

            zeros = jnp.zeros((8, D), F32)
            sums = (zeros, zeros)
            for index in range(4):
                sums = lax.fori_loop(index * 9, (index + 1) * 9, norm_step, sums, unroll=3)
                tick(base, index, back)
            for index in range(2):
                total = jnp.sum(sums[index], axis=0, keepdims=True)
                for part in range(3):
                    row = 3 * index + part
                    norm_parts[rank, row : row + 1, :] = total[:, part * CT : (part + 1) * CT]

            for mask in range(1, ranks):
                norm_copy(mask).start()
            pltpu.make_async_copy(normed_sum, grad_tokens, late_sems.at[9]).start()

        @pl.when((step > tiles) & (tile == 1))
        def _():
            for phase in range(4):
                for event in due[base + back + phase]:
                    event()

        @pl.when((step > tiles) & (tile == last))
        def _():
            chunk = other_held.shape[1]
            for stream, (_, lanes) in enumerate(other_exchange.cuts):
                for source in range(ranks):
                    row = pl.multiple_of(quarter * quarter_rows + source * chunk, 8)
                    slot = other_exchange.rank_slot(stream, source)
                    other_held[slot, :, lanes] = misc[stream, pl.ds(row, chunk), :]
            other_exchange.start()
            for phase in range(4):
                for event in due[base + last * back + phase]:
                    event()

        product(spec_kept.at[tile], source_spec, leaves, True)
        transform(table_back, leaves, parts)
        tick(base, 4, back)

        for side, three in ((0, three_f), (1, three_r)):
            for half in range(2):
                start = side * LONG + half * 512
                grad_total[start : start + 512, :] = dot(hidden_two[start : start + 512, :], three[...].astype(BF16))

        for half, lanes in enumerate(HALVES):

            def filter_step(index, carry, lanes=lanes):
                sums = []
                cyclic, negative = unfold_rows(parts, index * 16, lanes)
                for part in range(4):
                    place = index * 16 + LEAF * part
                    grads = (
                        (cyclic[part] + negative[part]) * 0.25,
                        (cyclic[part] - negative[part]) * 0.25,
                    )
                    for side, rate in ((0, rate_f), (1, rate_r)):
                        window, distance = window_rows(side, place, rate[:, lanes])
                        rows = rows_of(place + side * LONG, 16)
                        held = grad_total[rows, lanes]
                        out = grads[side] * window
                        grad_total[rows, lanes] = out
                        sums.append((held * out * distance).reshape(2, 8, 128).sum(0))
                return (
                    carry[0] + sums[0] + sums[2] + sums[4] + sums[6],
                    carry[1] + sums[1] + sums[3] + sums[5] + sums[7],
                )

            zeros = jnp.zeros((8, 128), F32)
            found = lax.fori_loop(0, LEAF // 16, filter_step, (zeros, zeros), unroll=2)
            for side in range(2):
                rate_sums[side, :, lanes] = found[side]
            tick(base, 5 + half, back)

        narrow = narrow_kept[tile]

        for side, rate, three, start, piece in (
            (0, rate_f, three_f, 0, narrow[:SHORT]),
            (1, rate_r, three_r, LONG - SHORT, narrow[SHORT:]),
        ):
            extra = jnp.sum(rate_sums[side], axis=0, keepdims=True)
            held = dot(hidden_two[side * LONG + start : side * LONG + start + SHORT, :], three[...].astype(BF16))
            for at in range(0, SHORT, 16):
                window, distance = window_rows(side, start + at, rate)
                grad = piece[at : at + 16]
                if side == 1 and at == 0:
                    first = lax.broadcasted_iota(jnp.int32, grad.shape, 0) == 0
                    grad = jnp.where(first, 0.0, grad)
                out = grad * window
                spot = side * LONG + start + at
                grad_total[spot : spot + 16, :] += out
                extra += jnp.sum(held[at : at + 16] * out * distance, axis=0, keepdims=True)
            for half in range(2):
                row = MISC_RATE + 2 * side + half
                misc[tile, row : row + 1, :] = -extra[:, half * 128 : (half + 1) * 128]

        for side, three in ((0, three_f), (1, three_r)):
            rows = slice(side * LONG, (side + 1) * LONG)
            low = grad_total[rows, :].astype(BF16)
            out = dot_tn(hidden_two[rows, :], low)
            for half in range(2):
                row = (2 * side + half) * ORDER
                misc[tile, row : row + ORDER, :] = out[:, half * 128 : (half + 1) * 128]
            deep = dot_nt(low, three[...].astype(BF16))

            @pl.when(tile == 0)
            def _():
                grad_deep[rows, :] = deep

            @pl.when(tile > 0)
            def _():
                grad_deep[rows, :] += deep

        tick(base, 7, back)

        @pl.when(tile < last)
        def _():
            tick(base, 8, back)

        @pl.when(tile == last)
        def _():
            two, shallow = None, []
            for side in range(2):
                lanes = slice(side * ORDER, (side + 1) * ORDER)
                deep = grad_deep[side * LONG : (side + 1) * LONG, :] * padded[2, 0:LONG, lanes]
                term = lax.dot_general(
                    padded[0, 0:LONG, lanes],
                    deep,
                    (((0,), (0,)), ((), ())),
                    precision=PRECISE,
                    preferred_element_type=F32,
                )
                two = term if side == 0 else two + term
                each = lax.dot_general(
                    deep, filter_two[...], (((1,), (1,)), ((), ())), precision=PRECISE, preferred_element_type=F32
                )
                shallow.append(each * padded[1, 0:LONG, lanes])
            misc[tile, MISC_TWO : MISC_TWO + ORDER, :] = two
            misc[tile, MISC_ONE : MISC_ONE + 8, :] = jnp.dot(
                features[...], jnp.concatenate(shallow, axis=0), precision=PRECISE, preferred_element_type=F32
            )
            misc_start()

        @pl.when(tile == last)
        def _():
            for event in due[base + last * back + 8]:
                event()
            if late:
                for event in late.pop(0):
                    event()
            misc_turn()
            for events in late:
                for event in events:
                    event()
            misc_finish()
            pltpu.make_async_copy(normed_sum, grad_tokens, late_sems.at[9]).wait()
            for mask in range(1, ranks):
                norm_copy(mask).wait()
            total = norm_parts[0]
            for index in range(1, ranks):
                total += norm_parts[index]
            norm_whole[...] = total


class Places:
    def __init__(self, ranks, quarters):
        self.ranks, self.bits = ranks, ranks.bit_length() - 1
        self.rank, self.quarter = lax.axis_index("dp"), lax.axis_index("tensor")
        rest, self.digits = self.rank, []
        for _ in range(self.bits):
            half = lax.div(rest, 2)
            self.digits.append(rest - 2 * half)
            rest = half
        turned = [(1 << bit) * (1 - 2 * digit) for bit, digit in enumerate(self.digits)]
        self.across = [self.rank]
        for mask in range(1, ranks):
            top = mask.bit_length() - 1
            self.across.append(self.across[mask - (1 << top)] + turned[top])
        z = self.quarter
        upper = lax.div(z, 2)
        self.origins = (z, z + 1 - 2 * (z - 2 * upper), 2 - upper, 3 * (1 - upper))


def up_to(value, unit):
    return -(-value // unit) * unit


def greet(places, everyone):
    barrier = pltpu.get_barrier_semaphore()
    peers = [mask for mask in range(1, places.ranks) if everyone or mask & (mask - 1) == 0]
    for mask in peers:
        pl.semaphore_signal(barrier, inc=1, device_id={"dp": places.across[mask]}, device_id_type=MESH)

    for origin in places.origins[1:]:
        pl.semaphore_signal(barrier, inc=1, device_id={"tensor": origin}, device_id_type=MESH)
    pl.semaphore_wait(barrier, len(peers) + len(places.origins) - 1)


def whole_shape(ranks, quarters, rows, lanes):
    split = (2,) * (ranks.bit_length() - 1) if ranks <= LOCAL else (ranks,)
    return (quarters, *split, rows, lanes)


class Exchange:
    def __init__(self, places, cuts, whole, sems, held=None, landed=None, own=None, line=True, relay=False, flush=None):
        self.places, self.bits, self.ranks = places, places.bits, places.ranks
        rest = list(range(1, self.bits))
        self.orders = ([0] + rest, [0] + rest[::-1])
        self.cuts, self.whole = cuts, whole
        self.held, self.landed = held, landed
        self.own = held.at[0] if own is None else own
        self.local_sems, self.sum_sems, self.cross_sems, self.line_sems, self.spread_sems = sems
        self.line, self.relay, self.flush = line, relay, flush
        self.origins = places.origins if line else (0,)

    @staticmethod
    def semaphores(ranks, quarters, lead=()):
        bits = ranks.bit_length() - 1
        kind = pltpu.SemaphoreType.DMA
        shapes = ((1 + quarters,), (2, 2, bits), (2, quarters), (5,), (2, 2, quarters, bits))
        return [kind(lead + shape) for shape in shapes]

    def mask(self, stream, slot):
        order = self.orders[stream]
        return sum(1 << order[self.bits - 1 - place] for place in range(self.bits) if slot >> place & 1)

    def slot_rank(self, stream, slot):
        return self.places.across[self.mask(stream, slot)]

    def rank_slot(self, stream, rank):
        slot = 0
        for place in range(self.bits):
            bit = self.orders[stream][self.bits - 1 - place]
            mine = self.places.digits[bit]
            slot = slot + (1 << place) * (1 - mine if rank >> bit & 1 else mine)
        return slot

    def spot(self, origin, mask=0):
        if self.ranks > LOCAL:
            return self.whole.at[origin, self.places.across[mask]]
        return self.whole.at[(origin, *self.places.digits[::-1])]

    def filled(self, stream, origin, j):
        order = self.orders[stream]
        known = [order[self.bits - 1 - step] for step in range(j)]
        index = [slice(None) if bit in known else self.places.digits[bit] for bit in reversed(range(self.bits))]
        return self.whole.at[(origin, *index, *self.cuts[stream])]

    def partner(self, bit):
        return {"dp": self.places.across[1 << bit]}

    def sum_copy(self, stream, k):
        half = self.ranks >> (k + 1)
        start = self.ranks - 2 * half
        rows, lanes = self.cuts[stream]
        return pltpu.make_async_remote_copy(
            src_ref=self.held.at[half : 2 * half, rows, lanes],
            dst_ref=self.landed.at[start : start + half, rows, lanes],
            send_sem=self.sum_sems.at[0, stream, k],
            recv_sem=self.sum_sems.at[1, stream, k],
            device_id=self.partner(self.orders[stream][k]),
            device_id_type=MESH,
        )

    def sum_start(self, k):
        for stream in range(2):
            self.sum_copy(stream, k).start()

    def sum_finish(self, k):
        half = self.ranks >> (k + 1)
        start = self.ranks - 2 * half
        for stream in range(2):
            self.sum_copy(stream, k).wait_recv()
            rows, lanes = self.cuts[stream]

            def add(index, carry, rows=rows, lanes=lanes):
                self.held[index, rows, lanes] += self.landed[start + index, rows, lanes]
                return carry

            lax.fori_loop(0, half, add, 0)

    def cross_copy(self, origin, index):
        spot = self.spot(origin)
        return pltpu.make_async_remote_copy(
            src_ref=self.own,
            dst_ref=spot,
            send_sem=self.cross_sems.at[0, index],
            recv_sem=self.cross_sems.at[1, origin],
            device_id={"tensor": self.places.origins[index]},
            device_id_type=MESH,
        )

    def cross_start(self):
        if self.relay:
            self.line_start(0)
            return
        for index in range(1, len(self.origins)):
            self.cross_copy(self.origins[0], index).start()

    def cross_finish(self, index):
        self.cross_copy(self.origins[index], index).wait_recv()
        if self.relay:
            self.line_start(index)

    def line_copy(self, origin, index, target):
        spot = self.spot(origin)
        return pltpu.make_async_remote_copy(
            src_ref=self.own if index < 2 else spot,
            dst_ref=spot,
            send_sem=self.line_sems.at[index],
            recv_sem=self.cross_sems.at[1, origin],
            device_id={"tensor": target},
            device_id_type=MESH,
        )

    def line_moves(self, index):
        z, last = self.places.quarter, len(self.origins) - 1
        if index == 0:
            return [(z < last, z, 0, z + 1), (z > 0, z, 1, z - 1)]
        origin = self.origins[index]
        return [
            ((origin < z) & (z < last), origin, 1 + index, z + 1),
            ((origin > z) & (z > 0), origin, 1 + index, z - 1),
        ]

    def line_start(self, index):
        for wanted, origin, sem, target in self.line_moves(index):

            @pl.when(wanted)
            def _(origin=origin, sem=sem, target=target):
                self.line_copy(origin, sem, target).start()

    def spread_part(self, stream, index, j, src, dst):
        return pltpu.make_async_remote_copy(
            src_ref=src,
            dst_ref=dst,
            send_sem=self.spread_sems.at[0, stream, index, j],
            recv_sem=self.spread_sems.at[1, stream, index, j],
            device_id=self.partner(self.orders[stream][self.bits - 1 - j]),
            device_id_type=MESH,
        )

    def spread_parts(self, stream, index, j):
        origin, cut = self.origins[index], self.cuts[stream]
        if j == 0:
            spot = self.spot(origin).at[cut]
            return [(self.own.at[cut] if index == 0 else spot, spot)]
        if self.ranks <= LOCAL:
            part = self.filled(stream, origin, j)
            return [(part, part)]
        spots = [self.spot(origin, self.mask(stream, slot)).at[cut] for slot in range(1 << j)]
        return [(spot, spot) for spot in spots]

    def spread_start(self, index, j):
        for stream in range(2):
            for src, dst in self.spread_parts(stream, index, j):
                self.spread_part(stream, index, j, src, dst).start()

    def spread_all(self, stream, index, j):
        if self.ranks <= LOCAL:
            part = self.filled(stream, self.origins[index], j)
        else:
            part = self.whole.at[(0, slice(0, 1 << j), *self.cuts[stream])]
        return self.spread_part(stream, index, j, part, part)

    def spread_finish(self, index, j):
        for stream in range(2):
            self.spread_all(stream, index, j).wait_recv()

    def own_copy(self):
        return pltpu.make_async_copy(self.own, self.spot(self.origins[0]), self.local_sems.at[0])

    def flush_copy(self, index):
        origin = self.origins[index]
        return pltpu.make_async_copy(self.whole.at[origin], self.flush.at[origin], self.local_sems.at[1 + index])

    def gather_start(self):
        self.own_copy().start()
        self.cross_start()
        self.spread_start(0, 0)

    def settle(self):
        if self.flush is not None:
            for index in range(len(self.origins)):
                self.flush_copy(index).wait()
        for stream in range(2):
            if self.held is not None:
                for k in range(self.bits):
                    self.sum_copy(stream, k).wait_send()
            for index in range(len(self.origins)):
                for j in range(self.bits):
                    self.spread_all(stream, index, j).wait_send()
        if not self.relay:
            for index in range(1, len(self.origins)):
                self.cross_copy(self.origins[0], index).wait_send()
            return
        for index in range(len(self.origins)):
            for wanted, origin, sem, target in self.line_moves(index):

                @pl.when(wanted)
                def _(origin=origin, sem=sem, target=target):
                    self.line_copy(origin, sem, target).wait_send()

    def start(self):
        if self.held is None:
            self.gather_start()
        else:
            self.sum_start(0)

    def levels(self):
        bits, ahead = self.bits, 0
        steps = []

        def put(level, step, *args):
            while len(steps) <= level:
                steps.append([])
            steps[level].append(functools.partial(step, *args))

        def summed(k):
            self.sum_finish(k)
            if k + 1 < bits:
                self.sum_start(k + 1)
            else:
                self.gather_start()

        if self.held is not None:
            ahead = bits
            for k in range(bits):
                put(k, summed, k)

        def arrive(index):
            self.cross_finish(index)
            self.spread_start(index, 0)

        def advance(index, j):
            self.spread_finish(index, j)
            if index == 0 and j == 0:
                self.own_copy().wait()
            if j + 1 < bits:
                self.spread_start(index, j + 1)
            elif self.flush is not None:
                self.flush_copy(index).start()

        for index in range(len(self.origins)):
            if index:
                put(ahead + (index - 1 if self.relay else 0), arrive, index)
            for j in range(bits):
                put(ahead + (index if self.relay else min(index, 1)) + j, advance, index, j)
        put(len(steps), self.settle)
        return steps


PASS = 32


def glu_kernel(
    tokens,
    cotangent,
    mixed,
    mixed_own,
    valid,
    out_weight,
    vectors,
    gathered,
    down_second,
    result,
    grad_hidden,
    grad_mixed,
    early,
    grad_out,
    gate_weight,
    up_weight,
    down_weight,
    second,
    hidden,
    unit,
    scale,
    normed,
    gate_mid,
    up_mid,
    slope,
    silu,
    inner,
    summed,
    grad_summed,
    grad_inner,
    gate_low,
    up_low,
    windows,
    branch,
    grad_down,
    grad_gate,
    grad_up,
    sums,
    norm_sums,
    down_ahead,
    down_back,
):
    step = pl.program_id(0)
    last = pl.num_programs(0) - 1
    count, own = mixed_own.shape
    width = second.shape[2]
    quarters = width // own
    gain, shift = vectors[GAIN_TWO : GAIN_TWO + 1, :], vectors[SHIFT_TWO : SHIFT_TWO + 1, :]

    @pl.when(step == 0)
    def _():
        for ref in (gate_weight, up_weight, down_weight):
            ref[...] = jnp.zeros(ref.shape, BF16)
        height = gathered.shape[0] // quarters
        starts = [lax.rem(lax.axis_index("tensor") + q, quarters) * height for q in range(quarters)]

        def piece(q, start, rows):
            return gathered[pl.ds(pl.multiple_of(starts[q] + start, 8), rows), :]

        for block in range(NB):
            rest = [piece(q, REST_AT[0] + block * DB, DB) for q in range(quarters)]
            for which, ref in enumerate((gate_weight, up_weight)):
                pieces = []
                for q in range(quarters):
                    pieces.append(piece(q, ROWS_AT[which] + block * DB, DB))
                    pieces.append(rest[q][:, 64 * which : 64 * which + 64])
                ref[block, WSKIP[block] : WSKIP[block] + DB, :] = jnp.concatenate(pieces, 1).astype(BF16)
            side, at = block // 2, block % 2
            for q in range(quarters):
                value = piece(q, ROWS_AT[2] + block * DB, DB)
                rest = piece(q, REST_AT[1] + at * DB, DB)[:, 64 * side : 64 * side + 64]
                down_weight[block, q * own : (q + 1) * own, 0:DB] = jnp.concatenate([value, rest], 1).astype(BF16)
        square = NB * NB
        rest = [piece(q, REST_AT[2], square) for q in range(quarters)]
        factors = []
        for which in range(2):
            pieces = []
            for q in range(quarters):
                pieces.append(piece(q, ROWS_AT[3] + which * square, square))
                pieces.append(rest[q][:, 64 * which : 64 * which + 64])
            factors.append(jnp.concatenate(pieces, 1))
        factors = jnp.concatenate(factors, 0)
        for index in range(2 * NB * NB):
            second[index] = jnp.broadcast_to(factors[index : index + 1], (8, width))
        down_ahead[...] = jnp.zeros(down_ahead.shape, F32)
        down_back[...] = jnp.zeros(down_back.shape, F32)
        for block in range(NB):
            for out in range(NB):
                factor = jnp.broadcast_to(down_second[block, out : out + 1, :], (8, DB))
                down_back[block * NB + out, :, 0:DB] = factor
                down_ahead[block * NB + out, :, WSKIP[out] : WSKIP[out] + DB] = factor
        for ref in (grad_down, grad_gate, grad_up, grad_out, sums, norm_sums):
            ref[...] = jnp.zeros(ref.shape, F32)

    hidden[...] = dot(mixed[...], out_weight[...]) + tokens[...].astype(F32)

    def norm_step(index, carry):
        rows = rows_of(index * PASS, PASS)
        x = hidden[rows, :]
        centre = x - jnp.mean(x, axis=1, keepdims=True)
        spread = jnp.mean(centre * centre, axis=1, keepdims=True)
        root = lax.rsqrt(spread + EPSILON)
        held = centre * root
        unit[rows, :] = held
        scale[rows, :] = jnp.broadcast_to(root, (PASS, 128))
        normed[rows, :] = (held * gain + shift).astype(BF16)
        return carry

    lax.fori_loop(0, count // PASS, norm_step, 0, unroll=3)

    for block in range(NB):
        window = normed[:, WBASE[block] : WBASE[block] + 256]
        gate_mid[block] = dot(window, gate_weight[block])
        up_mid[block] = dot(window, up_weight[block])

    def split(value):
        return value.reshape(PASS // 8, 8, 128)

    def joined(value):
        return value.reshape(PASS, 128)

    def ahead_lanes(tile, carry):
        lanes = pl.ds(pl.multiple_of(tile * 128, 128), 128)

        def ahead_rows(index, inside):
            rows = rows_of(index * PASS, PASS)
            mask = split(valid[rows, :])
            for out in range(NB):
                gate = up = None
                for block in range(NB):
                    term = split(gate_mid[block, rows, lanes]) * second[block * NB + out, :, lanes]
                    gate = term if gate is None else gate + term
                    term = split(up_mid[block, rows, lanes]) * second[NB * NB + block * NB + out, :, lanes]
                    up = term if up is None else up + term
                sigmoid = 0.5 * jnp.tanh(0.5 * gate) + 0.5
                passed = gate * sigmoid
                masked_up = mask * up
                inner[out, rows, lanes] = joined(passed * masked_up).astype(BF16)
                slope[out, rows, lanes] = joined(masked_up * (sigmoid + passed * (1.0 - sigmoid)))
                silu[out, rows, lanes] = joined(passed * mask)
            return inside

        lax.fori_loop(0, count // PASS, ahead_rows, 0, unroll=3)
        return carry

    lax.fori_loop(0, width // 128, ahead_lanes, 0)

    for block in range(NB):
        summed[block] = dot(inner[block], down_weight[block])

    def down_step(index, carry):
        rows = rows_of(index * 16, 16)
        incoming = cotangent[rows, :].astype(F32)
        fields = []
        for block in range(NB):
            field = incoming[:, WBASE[block] : WBASE[block] + 256]
            if WSKIP[block]:
                field = pltpu.roll(field, 256 - WSKIP[block], 1)
            fields.append(field.reshape(2, 8, 256))
        values = [summed[block, rows, :] for block in range(NB)]
        moved = [pltpu.roll(value, 64, 1).reshape(2, 8, 256) for value in values]
        values = [value.reshape(2, 8, 256) for value in values]
        outs = []
        for out in range(NB):
            chosen = moved if WSKIP[out] else values
            total = None
            for block in range(NB):
                term = chosen[block] * down_ahead[block * NB + out]
                total = term if total is None else total + term
            outs.append(total.reshape(16, 256))
        held = hidden[rows, :]
        tiles = []
        for pair in (0, 2):
            left, right = outs[pair], outs[pair + 1]
            tiles += [left[:, :128], left[:, 128:] + right[:, :128], right[:, 128:]]
        for tile, out in enumerate(tiles):
            lanes = slice(tile * 128, (tile + 1) * 128)
            result[rows, lanes] = held[:, lanes] + out
        for block in range(NB):
            total = None
            for out in range(NB):
                term = fields[out] * down_back[block * NB + out]
                total = term if total is None else total + term
                sums[2 * NB * NB + block * NB + out] += (fields[out] * values[block]).sum(0)
            grad_summed[block, rows, :] = total.reshape(16, 256).astype(BF16)
        return carry

    lax.fori_loop(0, count // 16, down_step, 0, unroll=2)

    for block in range(NB):
        grad_inner[block] = dot_nt(grad_summed[block], down_weight[block])
        grad_down[block] += dot_tn(inner[block, :, 0:256], grad_summed[block])

    def back_rows(lanes, keep):
        def run(index, inside):
            rows = rows_of(index * PASS, PASS)
            grads = [split(grad_inner[block, rows, lanes]) for block in range(NB)]
            for which, factor, middle, low in (
                (0, slope, gate_mid, gate_low),
                (NB * NB, silu, up_mid, up_low),
            ):
                terms = [grads[block] * split(factor[block, rows, lanes]) for block in range(NB)]
                for block in range(NB):
                    total = None
                    for out in range(NB):
                        term = terms[out] * second[which + block * NB + out, :, lanes]
                        total = term if total is None else total + term
                    low[block, rows, lanes] = joined(total).astype(BF16)
                    if keep:
                        held = split(middle[block, rows, lanes])
                        for out in range(NB):
                            sums[which + block * NB + out, :, lanes] += (held * terms[out]).sum(0)
            return inside

        lax.fori_loop(0, count // PASS, run, 0, unroll=3)

    kept = -(-own // 128)
    for tile in range(kept):
        back_rows(slice(tile * 128, (tile + 1) * 128), True)

    def back_lanes(tile, carry):
        back_rows(pl.ds(pl.multiple_of(tile * 128, 128), 128), False)
        return carry

    lax.fori_loop(kept, width // 128, back_lanes, 0)

    for block in range(NB):
        windows[block] = dot_nt(gate_low[block], gate_weight[block]) + dot_nt(
            up_low[block], up_weight[block]
        )
        window = normed[:, WBASE[block] : WBASE[block] + 256]
        grad_gate[block] += dot_tn(window, gate_low[block, :, 0:256])
        grad_up[block] += dot_tn(window, up_low[block, :, 0:256])

    def norm_back(index, carry):
        rows = rows_of(index * PASS, PASS)
        pieces = []
        for pair in (0, 2):
            left, right = windows[pair, rows, :], windows[pair + 1, rows, :]
            pieces += [left[:, :128], left[:, 128:] + right[:, :128], right[:, 128:]]
        grad = jnp.concatenate(pieces, axis=1)
        held = unit[rows, :]
        norm_sums[0] += (grad * held).reshape(PASS // 8, 8, D).sum(0)
        norm_sums[1] += grad.reshape(PASS // 8, 8, D).sum(0)
        wide = grad * gain
        mean = jnp.mean(wide, axis=1, keepdims=True)
        along = jnp.mean(wide * held, axis=1, keepdims=True)
        out = cotangent[rows, :].astype(F32) + scale[rows, 0:1] * (wide - mean - held * along)
        grad_hidden[rows, :] = out
        branch[rows, :] = out.astype(BF16)
        return carry

    lax.fori_loop(0, count // PASS, norm_back, 0, unroll=3)

    grad_mixed[...] = dot_nt(branch[...], out_weight[...]).astype(BF16)
    grad_out[0:own, :] += dot_tn(mixed_own[...], branch[...])

    @pl.when(step == last)
    def _():
        early[ROWS_AT[4] :, :] = jnp.zeros((early.shape[0] - ROWS_AT[4], 128), F32)
        for block in range(NB):
            skip, start = WSKIP[block], block * DB
            pairs = [ref[block, skip : skip + DB, 0:own] for ref in (grad_gate, grad_up)]
            for which, value in enumerate(pairs):
                early[ROWS_AT[which] + start : ROWS_AT[which] + start + DB, :] = value[:, 0:128]
            early[REST_AT[0] + start : REST_AT[0] + start + DB, :] = jnp.concatenate(
                [value[:, 128:] for value in pairs], axis=1
            )
            early[ROWS_AT[2] + start : ROWS_AT[2] + start + DB, :] = grad_down[block, 0:own, 0:128]
        for block in range(2):
            start = REST_AT[1] + block * DB
            early[start : start + DB, :] = jnp.concatenate(
                [grad_down[side, 0:own, 128:DB] for side in (block, block + 2)], axis=1
            )
        square = NB * NB
        small = jnp.sum(sums[...], axis=1)
        early[ROWS_AT[3] : ROWS_AT[4], :] = small[:, 0:128]
        early[REST_AT[2] : REST_AT[2] + square, :] = jnp.concatenate(
            [small[0:square, 128:192], small[square : 2 * square, 128:192]], axis=1
        )
        early[REST_AT[2] + square : REST_AT[2] + 2 * square, 0:64] = small[2 * square :, 128:192]
        norm = jnp.sum(norm_sums[...], axis=1)
        for index in range(2 * D // 128):
            which, at = index // (D // 128), index % (D // 128) * 128
            early[ROWS_AT[4] + index : ROWS_AT[4] + index + 1, :] = norm[which : which + 1, at : at + 128]


GLU_ROWS = 288


def vmem_specs(shapes):
    return [pltpu.VMEM(shape, kind) for shape, kind in shapes]


def whole_spec(array):
    return pl.BlockSpec(array.shape, lambda step, rank=array.ndim: (0,) * rank)


def column_spec(rows, at=0, width=CT):
    return pl.BlockSpec((rows, width), lambda step, at=at: (0, step + at))


def params():
    return pltpu.CompilerParams(dimension_semantics=("arbitrary",), vmem_limit_bytes=60 * MIB)


def spec_block():
    return pl.BlockSpec((4, 512, CT), lambda step: (0, 0, step))


def any_spec():
    return pl.BlockSpec(memory_space=pl.ANY)


def collective(index):
    return pltpu.CompilerParams(
        dimension_semantics=("arbitrary",),
        vmem_limit_bytes=63 * MIB,
        collective_id=index,
        has_side_effects=True,
    )


def tile_operands(in_weight, taps, three, tables):
    tiles = D // CT
    args = [in_weight] * 3 + [taps] * 3 + [three] * 2 + list(tables)
    specs = []
    for rows in (D, 3):
        specs += [column_spec(rows, at) for at in (0, tiles, 2 * tiles)]
    specs += [column_spec(ORDER, at) for at in (0, tiles)]
    return args, specs + [whole_spec(table) for table in tables]


def short_spec():
    return pl.BlockSpec((2, 2 * SHORT, CT), lambda step: (0, 0, step))


def mixer_forward(ranks, quarters, lengths, singles, filters, weights, tokens, features, operands):
    args, specs = tile_operands(*operands)
    height = up_to(PACKED, 8 * ranks)
    shape = jax.ShapeDtypeStruct
    outs = (
        [shape((TOK, D), BF16)] * 5
        + [shape((4, 512, D), BF16)] * 2
        + [shape((2 * SHORT, D), F32), shape((2, 2 * SHORT, D), F32), shape((TOK, D), BF16)]
        + [shape(whole_shape(ranks, quarters, height // ranks, 128), F32)]
        + [shape((TOK, 128), F32), shape((8, D), F32), shape((2 * LONG, ORDER), F32)]
        + [shape((2 * LONG, 3 * ORDER), BF16)]
        + [shape((2 * LONG, ORDER), F32)] * 2
        + [shape((TOK, D // quarters), BF16)] * 2
    )
    out_specs = [column_spec(TOK)] * 5 + [spec_block()] * 2
    out_specs += [column_spec(2 * SHORT), short_spec(), whole_spec(outs[9]), any_spec()]
    out_specs += [whole_spec(each) for each in outs[11:]]
    scratch = [
        ((3, PADROWS, CT), F32),
        ((TOK, CT), F32),
        ((TOK, CT), F32),
        ((2, LONG, CT), F32),
        ((4, 512, CT), BF16),
        ((4, 512, CT), F32),
        ((4, 512, CT), F32),
        ((height, 128), F32),
        (outs[10].shape if ranks <= LOCAL else (8, 128), F32),
    ]

    def kernel(*refs):
        singles_in, refs = refs[1 : 1 + len(singles)], refs[:1] + refs[1 + len(singles) :]
        filters_in, refs = refs[1 : 1 + len(filters)], refs[:1] + refs[1 + len(filters) :]
        weights_in, refs = refs[1 : 1 + len(weights)], refs[:1] + refs[1 + len(weights) :]
        mixer_forward_kernel(ranks, quarters, refs[0], singles_in, filters_in, weights_in, *refs[1:])

    wholes = [*singles, *filters, *weights, tokens]
    return pl.pallas_call(
        kernel,
        grid=(D // CT,),
        in_specs=[pl.BlockSpec(memory_space=pltpu.SMEM)]
        + [whole_spec(each) for each in wholes]
        + specs
        + [whole_spec(features)],
        out_specs=out_specs,
        out_shape=outs,
        scratch_shapes=vmem_specs(scratch) + Exchange.semaphores(ranks, quarters),
        compiler_params=collective(0),
        cost_estimate=pl.CostEstimate(flops=12_000_000_000, bytes_accessed=40_000_000, transcendentals=2_000_000),
        name="mixer_forward",
    )(lengths, *wholes, *args, features)


def mixer_backward(
    ranks, quarters, early, grad_out, tokens, valid, vectors, hidden_two, operands, saved, grad_mixed, normed_own, late
):
    tiles = D // CT
    in_weight, taps, three, tables = operands
    total, *masked, kernel_spec, source_spec, kernel_short, source_short = saved

    def ahead(rows, at=0):
        return pl.BlockSpec((rows, CT), lambda step, at=at: (0, jnp.minimum(step, tiles - 1) + at))

    def behind(rows, at=0):
        return pl.BlockSpec((rows, CT), lambda step, at=at: (0, jnp.maximum(step - tiles, 0) + at))

    args = [early, grad_out, tokens, valid, vectors, hidden_two]
    specs = [any_spec()] * 3 + [whole_spec(valid), whole_spec(vectors)]
    specs += [pl.BlockSpec((2 * LONG, ORDER), lambda step: (0, 0))]
    args += [in_weight] * 3 + [taps] * 3 + [three] * 2 + list(tables)
    for rows in (D, 3):
        specs += [ahead(rows, at) for at in (0, tiles, 2 * tiles)]
    specs += [behind(ORDER, at) for at in (0, tiles)] + [whole_spec(table) for table in tables]
    args += [total, *masked, kernel_spec, source_spec, kernel_short, source_short, grad_mixed, normed_own, *late]
    specs += [pl.BlockSpec((TOK, CT), lambda step: (0, jnp.minimum(step, tiles - 1)), pipeline_mode=pl.Buffered(1))]
    specs += [ahead(TOK)] * 3
    specs += [pl.BlockSpec((4, 512, CT), lambda step: (0, 0, jnp.minimum(step, tiles - 1)), pipeline_mode=pl.Buffered(1))]
    specs += [pl.BlockSpec((4, 512, CT), lambda step: (0, 0, jnp.maximum(step - tiles, 0)), pipeline_mode=pl.Buffered(1))]
    specs += [ahead(2 * SHORT)]
    specs += [pl.BlockSpec((2, 2 * SHORT, CT), lambda step: (0, 0, jnp.minimum(step, tiles - 1)))]
    specs += [ahead(TOK), whole_spec(normed_own)] + [any_spec()] * 4 + [whole_spec(each) for each in late[4:]]
    early_rows = early.shape[0] // ranks
    chunk = grad_out.shape[0] // ranks
    shape = jax.ShapeDtypeStruct
    outs = [
        shape((TOK, D), F32),
        shape(whole_shape(ranks, 1, early_rows, 128), F32),
        shape(whole_shape(ranks, quarters, chunk, D), F32),
        shape((tiles, *whole_shape(ranks, quarters, chunk, D)), F32),
        shape(whole_shape(ranks, quarters, chunk, 256), F32),
        shape((8, CT), F32),
        shape((ranks, up_to(MISC_ROWS // ranks, 8), 128), F32),
    ]
    local = ranks <= LOCAL
    scratch = [
        ((3, PADROWS, CT), F32),
        ((3, PADROWS, CT), F32),
        ((2 * LONG, CT), F32),
        ((2, TOK, CT), BF16),
        ((4, 512, CT), BF16),
        ((4, 512, CT), F32),
        ((TOK, 3 * CT), BF16),
        ((TOK, D), F32),
        ((2 * LONG, ORDER), F32),
        ((3, max(quarters * ranks * chunk, ranks * outs[6].shape[1]), 128), F32),
        ((3, ranks, chunk, D), F32),
        ((3, ranks - 1, chunk, D), F32),
        ((3, *outs[2].shape) if local else (8, 128), F32),
        ((ranks, early_rows, 128), F32),
        ((ranks - 1, early_rows, 128), F32),
        (outs[1].shape if local else (8, 128), F32),
        ((ranks, chunk, 256), F32),
        ((ranks - 1, chunk, 256), F32),
        (outs[4].shape if local else (8, 128), F32),
        ((tiles, 4, 512, CT), BF16),
        ((tiles, 2 * SHORT, CT), F32),
        ((2, 8, CT), F32),
        ((ranks, 8, CT), F32),
        (outs[6].shape, F32),
        (outs[6].shape[1:], F32),
        (outs[6].shape, F32),
    ]
    dma = pltpu.SemaphoreType.DMA
    sems = [dma((4 * ranks,)), dma((11,)), dma((2, ranks - 1)), dma((2, 2, ranks - 1))]
    for lead in ((), (), (), (tiles,)):
        sems += Exchange.semaphores(ranks, quarters, lead)
    return pl.pallas_call(
        functools.partial(mixer_backward_kernel, ranks, quarters),
        grid=(2 * tiles,),
        in_specs=specs,
        out_specs=[any_spec()] * 5 + [whole_spec(each) for each in outs[5:]],
        out_shape=outs,
        scratch_shapes=vmem_specs(scratch) + sems,
        compiler_params=collective(1),
        cost_estimate=pl.CostEstimate(flops=14_000_000_000, bytes_accessed=40_000_000, transcendentals=2_000_000),
        name="mixer_backward",
    )(*args)


def glu(ranks, quarters, tokens, cotangent, mixed, mixed_own, valid, out_weight, vectors, gathered, down_second):
    own = mixed_own.shape[1]
    width = quarters * own
    count = GLU_ROWS
    shape = jax.ShapeDtypeStruct

    def tile(columns):
        return pl.BlockSpec((count, columns), lambda step: (step, 0))

    outs = [
        shape((TOK, D), F32),
        shape((TOK, D), F32),
        shape((TOK, D), BF16),
        shape((gathered.shape[0] // quarters, 128), F32),
        shape((up_to(D // quarters, 8 * ranks), D), F32),
    ]
    scratch = [
        ((NB, 256, width), BF16),
        ((NB, 256, width), BF16),
        ((NB, width, 256), BF16),
        ((2 * NB * NB, 8, width), F32),
        ((count, D), F32),
        ((count, D), F32),
        ((count, 128), F32),
        ((count, D), BF16),
        ((NB, count, width), F32),
        ((NB, count, width), F32),
        ((NB, count, width), F32),
        ((NB, count, width), F32),
        ((NB, count, width), BF16),
        ((NB, count, 256), F32),
        ((NB, count, 256), BF16),
        ((NB, count, width), F32),
        ((NB, count, width), BF16),
        ((NB, count, width), BF16),
        ((NB, count, 256), F32),
        ((count, D), BF16),
        ((NB, 256, 256), F32),
        ((NB, 256, 256), F32),
        ((NB, 256, 256), F32),
        ((3 * NB * NB, 8, 256), F32),
        ((2, 8, D), F32),
        ((NB * NB, 8, 256), F32),
        ((NB * NB, 8, 256), F32),
    ]
    whole = (out_weight, vectors, gathered, down_second)
    return pl.pallas_call(
        glu_kernel,
        grid=(TOK // count,),
        in_specs=[tile(D), tile(D), tile(D), tile(own), tile(128)] + [whole_spec(each) for each in whole],
        out_specs=[tile(D)] * 3 + [whole_spec(each) for each in outs[3:]],
        out_shape=outs,
        scratch_shapes=vmem_specs(scratch),
        compiler_params=params(),
        cost_estimate=pl.CostEstimate(flops=14_000_000_000, bytes_accessed=40_000_000, transcendentals=4_000_000),
        name="glu",
    )(tokens, cotangent, mixed, mixed_own, valid, *whole)


def unpack_kernel(
    quarters,
    grad_tokens,
    early,
    out_whole,
    tile_whole,
    other,
    norm,
    misc,
    tokens_out,
    in_out,
    out_out,
    three_out,
    two_out,
    gate_out,
    up_out,
    down_out,
    taps_out,
    one_out,
    gate_second_out,
    up_second_out,
    down_second_out,
    skip_out,
    rate_out,
    gain_out,
    shift_out,
    gain_two_out,
    shift_two_out,
    tokens_held,
    early_held,
    out_held,
    tile_held,
    load_sems,
    store_sems,
):
    tiles = D // CT
    stride = out_whole.shape[0] // quarters
    rows = D // quarters
    loads = [(tile_whole.at[job], tile_held.at[job]) for job in range(tiles)]
    loads += [(early, early_held), (out_whole, out_held), (grad_tokens, tokens_held)]
    loads = [pltpu.make_async_copy(src, dst, load_sems.at[index]) for index, (src, dst) in enumerate(loads)]
    for load in loads:
        load.start()

    groups = []
    for job in range(tiles):
        moves = []
        for part in range(3):
            at = part * D + job * CT
            for q in range(quarters):
                source = tile_held.at[job, q * stride : q * stride + rows, part * CT : (part + 1) * CT]
                moves.append((source, in_out.at[q * rows : (q + 1) * rows, at : at + CT]))
        for side in range(4):
            at = side // 2 * D + job * CT + side % 2 * 128
            rows_in = slice(side * ORDER, (side + 1) * ORDER)
            source = misc.at[rows_in] if job == tiles - 1 else other.at[rows_in, job * 128 : (job + 1) * 128]
            moves.append((source, three_out.at[:, at : at + 128]))
        if job == tiles - 1:
            moves.append((misc.at[MISC_TWO : MISC_TWO + ORDER], two_out))
        groups.append(moves)
    groups.append([])
    moves = []
    for q in range(quarters):
        moves.append((out_held.at[q * stride : q * stride + rows], out_out.at[q * rows : (q + 1) * rows]))
    groups.append(moves)
    groups.append([(tokens_held, tokens_out)])
    stores = []
    for load, moves in zip(loads, groups):
        load.wait()
        for source, target in moves:
            stores.append(pltpu.make_async_copy(source, target, store_sems.at[len(stores)]))
            stores[-1].start()

    for job in range(tiles):
        late = misc[MISC_TAPS:MISC_TWO, :]
        if job < tiles - 1:
            late = other[MISC_TAPS:MISC_TWO, job * 128 : (job + 1) * 128]
        for half in range(2):
            at = job * CT + half * 128
            taps = late[16 * half : 16 * half + 16]
            for part in range(3):
                taps_out[:, part * D + at : part * D + at + 128] = taps[3 * part : 3 * part + 3, :]
            skip_out[at : at + 128] = late[MISC_SKIP - MISC_TAPS + half]
            for side in range(2):
                rate_out[side * D + at : side * D + at + 128] = late[MISC_RATE - MISC_TAPS + 2 * side + half]
    one_out[...] = misc[MISC_ONE : MISC_ONE + one_out.shape[0], :]
    for block in range(NB):
        rest = early_held[REST_AT[0] + block * DB : REST_AT[0] + (block + 1) * DB, :]
        for which, out in enumerate((gate_out, up_out)):
            start = ROWS_AT[which] + block * DB
            out[block, :, 0:128] = early_held[start : start + DB, :]
            out[block, :, 128:] = rest[:, 64 * which : 64 * which + 64]
        start, at = ROWS_AT[2] + block * DB, REST_AT[1] + block % 2 * DB
        down_out[block, :, 0:128] = early_held[start : start + DB, :]
        down_out[block, :, 128:] = early_held[at : at + DB, :][:, 64 * (block // 2) : 64 * (block // 2) + 64]
    square = NB * NB
    for index, out in enumerate((gate_second_out, up_second_out, down_second_out)):
        start, at = ROWS_AT[3] + index * square, REST_AT[2] + index // 2 * square
        value = jnp.concatenate(
            [early_held[start : start + square, :], early_held[at : at + square, :][:, 64 * (index % 2) :][:, 0:64]], 1
        )
        for block in range(NB):
            out[block] = value[block * NB : (block + 1) * NB, :]
    for index, out in enumerate((gain_out, shift_out)):
        for part in range(3):
            out[part * CT : (part + 1) * CT] = norm[3 * index + part, :]
    for index, out in enumerate((gain_two_out, shift_two_out)):
        for at in range(D // 128):
            out[at * 128 : (at + 1) * 128] = early_held[ROWS_AT[4] + index * (D // 128) + at, :]
    for store in stores:
        store.wait()


def unpack(quarters, own, taken):
    shape = jax.ShapeDtypeStruct
    large = [
        shape((TOK, D), F32),
        shape((D, 3 * D), F32),
        shape((D, D), F32),
        shape((ORDER, 2 * D), F32),
        shape((ORDER, ORDER), F32),
    ]
    small = [
        shape((NB, DB, own), F32),
        shape((NB, DB, own), F32),
        shape((NB, own, DB), F32),
        shape((3, 3 * D), F32),
        shape((5, ORDER), F32),
        shape((NB, NB, own), F32),
        shape((NB, NB, own), F32),
        shape((NB, NB, DB), F32),
        shape((D,), F32),
        shape((2 * D,), F32),
    ] + [shape((D,), F32)] * 4
    tiles = D // CT
    copies = 2 + tiles * (3 * quarters + 4) + quarters
    vmem = pl.BlockSpec(memory_space=pltpu.VMEM)
    dma = pltpu.SemaphoreType.DMA
    return pl.pallas_call(
        functools.partial(unpack_kernel, quarters),
        in_specs=[any_spec()] * 4 + [vmem] * 3,
        out_specs=[any_spec()] * len(large) + [vmem] * len(small),
        out_shape=large + small,
        scratch_shapes=vmem_specs([(each.shape, F32) for each in taken[:4]]) + [dma((tiles + 3,)), dma((copies,))],
        compiler_params=pltpu.CompilerParams(vmem_limit_bytes=60 * MIB),
        cost_estimate=pl.CostEstimate(flops=0, bytes_accessed=30_000_000, transcendentals=0),
        name="unpack",
    )(*taken)


def body(
    tokens,
    lengths,
    gain_mix,
    shift_mix,
    in_weight,
    short_kernel,
    skip_gain,
    decay_rate,
    filter_one,
    filter_two,
    filter_three,
    out_weight,
    gain_ffn,
    shift_ffn,
    gate_first,
    gate_second,
    up_first,
    up_second,
    down_first,
    down_second,
    cotangent,
):
    ranks, quarters = lax.axis_size("dp"), lax.axis_size("tensor")
    tables = [jnp.asarray(each) for each in transforms()]
    features = filter_features()
    operands = (in_weight, short_kernel, filter_three, tables)
    (
        mixed,
        total,
        *masked,
        kernel_spec,
        source_spec,
        kernel_short,
        source_short,
        normed,
        gathered,
        valid,
        vectors,
        hidden_one,
        hidden_two,
        cos_one,
        cos_two,
        mixed_own,
        normed_own,
    ) = mixer_forward(
        ranks,
        quarters,
        lengths,
        (gain_mix, shift_mix, skip_gain, decay_rate, gain_ffn, shift_ffn),
        (filter_one, filter_two),
        (gate_first, up_first, down_first, gate_second, up_second),
        tokens,
        jnp.asarray(np.pad(features, ((0, 0), (0, 3)))),
        operands,
    )
    gathered = gathered.reshape(-1, 128)
    result, grad_hidden, grad_mixed, early, grad_out = glu(
        ranks, quarters, tokens, cotangent, mixed, mixed_own, valid, out_weight, vectors, gathered, down_second
    )
    taken = mixer_backward(
        ranks,
        quarters,
        early,
        grad_out,
        tokens,
        valid,
        vectors,
        hidden_two,
        operands,
        (total, *masked, kernel_spec, source_spec, kernel_short, source_short),
        grad_mixed,
        normed_own,
        (
            grad_hidden,
            hidden_one,
            cos_one,
            cos_two,
            filter_two,
            jnp.asarray(np.pad(features.T, ((0, 3), (0, 0)))),
        ),
    )
    grad_tokens, early, grad_out, tiles, other, norm, misc = taken
    taken = (
        grad_tokens,
        early.reshape(-1, 128),
        grad_out.reshape(-1, D),
        tiles.reshape(tiles.shape[0], -1, tiles.shape[-1]),
        other.reshape(-1, 256),
        norm,
        misc.reshape(-1, 128),
    )
    (
        grad_tokens,
        grad_in,
        grad_out,
        grad_three,
        grad_two,
        grad_gate,
        grad_up,
        grad_down,
        grad_taps,
        grad_one,
        grad_gate_second,
        grad_up_second,
        grad_down_second,
        grad_skip,
        grad_rate,
        grad_gain,
        grad_shift,
        grad_gain_two,
        grad_shift_two,
    ) = unpack(quarters, gate_first.shape[2], taken)
    return (
        result,
        grad_tokens,
        grad_gain,
        grad_shift,
        grad_in,
        grad_taps,
        grad_skip,
        grad_rate,
        grad_one,
        grad_two,
        grad_three,
        grad_out,
        grad_gain_two,
        grad_shift_two,
        grad_gate,
        grad_gate_second,
        grad_up,
        grad_up_second,
        grad_down,
        grad_down_second,
    )


def solution(mesh):
    split = (P(None, None, "tensor"),) * 4 + (P(None, "tensor", None),)
    return jax.shard_map(
        body,
        mesh=mesh,
        in_specs=(P("dp", None), P("dp")) + (P(),) * 12 + split + (P(), P("dp", None)),
        out_specs=(P("dp", None),) * 2 + (P(),) * 12 + split + (P(),),
        check_vma=False,
    )
```

profile of v0, /device:TPU:0, one launch (start us, length us, event | category | flops | bytes accessed | tf_op | source)
XLA Modules:
  0.0 290.6 jit_solution(1265314058686859807)
XLA Ops:
  0.7 74.0 %mixer_forward.1 = (bf16[1152,768]{1,0:T(8,128)(2,1)}, bf16[1152,768]{1,0:T(8,128)(2,1)}, bf16[1152,768]{1,0:T(8,128)(2,1)}, bf16[1152,768]{1,0:T(8,128)(2,1)}, ...) custom-call(s32[3]{0:T(128)} %refs_0_.1, ...), custom_call_target="tpu_custom_call" | custom-call | flops 12000000000 | bytes 40000000 | tf_op jit(solution)/shard_map/mixer_forward/pallas_call | solution.py:1750
  74.7 69.0 %glu.1 = (f32[1152,768]{1,0:T(8,128)}, f32[1152,768]{1,0:T(8,128)}, bf16[1152,768]{1,0:T(8,128)(2,1)}, f32[3584,128]{1,0:T(8,128)}, f32[192,768]{1,0:T(8,128)}) custom-call(bf16[1152,768]{1,0:T(8,128)(2,1)} %tokens.3, bf16[1152,768]{1,0:T(8,128)(2,1)} %cotangent.1, bf16[1152,768]{1,0:T(8,128)(2,1)} %get-tuple-element.69.mixed, ...), custom_call_target="tpu_custom_call" | custom-call | flops 14000000000 | bytes 40000000 | tf_op jit(solution)/shard_map/glu/pallas_call | solution.py:1898
  143.6 133.7 %mixer_backward.1 = (f32[1152,768]{1,0:T(8,128)}, f32[1,2,2,2,448,128]{5,4,3,2,1,0:T(8,128)}, f32[4,2,2,2,24,768]{5,4,3,2,1,0:T(8,128)}, f32[3,4,2,2,2,24,768]{6...) custom-call(f32[3584,128]{1,0:T(8,128)} %get-tuple-element.75.early, ...), custom_call_target="tpu_custom_call" | custom-call | flops 14000000000 | bytes 40000000 | tf_op jit(solution)/shard_map/mixer_backward/pallas_call | solution.py:1839
  277.3 13.1 %unpack.1 = (f32[1152,768]{1,0:T(8,128)}, f32[768,2304]{1,0:T(8,128)}, f32[768,768]{1,0:T(8,128)}, f32[128,1536]{1,0:T(8,128)}, f32[128,128]{1,0:T(8,128)}, /*in...) custom-call(f32[1152,768]{1,0:T(8,128)} %get-tuple-element.92.grad_t, ...), custom_call_target="tpu_custom_call" | custom-call | bytes 30000000 | tf_op jit(solution)/shard_map/unpack/pallas_call | solution.py:2049
where the time goes:
time: 291 us
  Pallas kernels  290 us (100%)
    pallas_call x1, Pallas kernels, mixer_backward(): pl.pallas_call(functools.partial(mixer_backward_kernel, ranks, quarters),...  134 us
    pallas_call x1, Pallas kernels, mixer_forward(): pl.pallas_call(kernel, grid=(D // CT,), in_specs=[pl.BlockSpec(memory_spa...  74 us
    pallas_call x1, Pallas kernels, glu(): pl.pallas_call(glu_kernel, grid=(TOK // count,), in_specs=[tile(D), tile(...  69 us
    pallas_call x1, Pallas kernels, unpack(): pl.pallas_call(functools.partial(unpack_kernel, quarters), in_specs=[any_...  13.1 us

commit v1 on v0

--- a/solution.py
+++ b/solution.py
@@ -198,33 +198,31 @@
 
 
 def transform(table, leaves, out):
-    def step(leaf, carry):
+    for leaf in range(4):
         out[leaf] = dot(table[leaf], leaves[leaf]).astype(out.dtype)
-        return carry
-
-    lax.fori_loop(0, 4, step, 0)
 
 
 def product(left, right, out, conjugate):
-    steps = LEAF // 16
-
-    def step(index, carry):
-        leaf = lax.div(index, steps)
-        place = (index - leaf * steps) * 16
-        real, imag = rows_of(place, 16), rows_of(place + LEAF, 16)
-        a, b = left[leaf, real, :].astype(F32), left[leaf, imag, :].astype(F32)
-        c, d = right[leaf, real, :].astype(F32), right[leaf, imag, :].astype(F32)
-        ac, bd = a * c, b * d
-        if conjugate:
-            new_real, new_imag = ac + bd, b * c - a * d
-        else:
-            new_real, new_imag = ac - bd, a * d + b * c
-        edge = (lax.broadcasted_iota(jnp.int32, a.shape, 0) + index * 16) == 0
-        out[leaf, real, :] = jnp.where(edge, ac, new_real).astype(BF16)
-        out[leaf, imag, :] = jnp.where(edge, bd, new_imag).astype(BF16)
-        return carry
-
-    lax.fori_loop(0, 4 * steps, step, 0, unroll=4)
+    for leaf in range(4):
+
+        def step(index, carry, leaf=leaf):
+            real, imag = rows_of(index * 16, 16), rows_of(index * 16 + LEAF, 16)
+            a, b = left[leaf, real, :].astype(F32), left[leaf, imag, :].astype(F32)
+            c, d = right[leaf, real, :].astype(F32), right[leaf, imag, :].astype(F32)
+            ac, bd = a * c, b * d
+            if conjugate:
+                new_real, new_imag = ac + bd, b * c - a * d
+            else:
+                new_real, new_imag = ac - bd, a * d + b * c
+            if leaf == 0:
+                edge = (lax.broadcasted_iota(jnp.int32, a.shape, 0) + index * 16) == 0
+                new_real = jnp.where(edge, ac, new_real)
+                new_imag = jnp.where(edge, bd, new_imag)
+            out[leaf, real, :] = new_real.astype(BF16)
+            out[leaf, imag, :] = new_imag.astype(BF16)
+            return carry
+
+        lax.fori_loop(0, LEAF // 16, step, 0, unroll=4)
 
 
 def product_short(left, right, conjugate):
@@ -298,20 +296,29 @@
     parts,
     flat,
     filling,
+    flat_sems,
     *sems,
 ):
     tile = pl.program_id(0)
     places = Places(ranks, quarters)
-    rows = flat.shape[0] // ranks
+    share = flat.shape[0] // ranks
     exchange = Exchange(
         places,
-        early_cuts(rows, 128),
+        early_cuts(share, 128),
         filling if ranks <= LOCAL else gathered,
         sems,
-        own=flat.at[pl.ds(pl.multiple_of(places.rank * rows, 8), rows)],
+        own=flat.at[pl.ds(pl.multiple_of(places.rank * share, 8), share)],
         relay=True,
         flush=gathered if ranks <= LOCAL else None,
     )
+    def own_quarter():
+        copies = []
+        for other in range(ranks):
+            spot = [other >> bit & 1 for bit in reversed(range(places.bits))] if ranks <= LOCAL else [other]
+            target = gathered.at[(places.quarter, *spot)]
+            copies.append(pltpu.make_async_copy(flat.at[other * share : (other + 1) * share], target, flat_sems.at[other]))
+        return copies
+
     phases = 5
     levels = exchange.levels()
 
@@ -352,6 +359,8 @@
             flat[start : start + DB, :] = jnp.concatenate(
                 [down[side].astype(F32)[:, 128:] for side in (block, block + 2)], axis=1
             )
+        for copy in own_quarter():
+            copy.start()
         greet(places, False)
         exchange.start()
 
@@ -401,7 +410,7 @@
             normed[rows, :] = out.astype(BF16)
             return carry
 
-        lax.fori_loop(0, TOK // 32, step, 0, unroll=4)
+        lax.fori_loop(0, TOK // 32, step, 0, unroll=6)
         for q in range(quarters):
 
             @pl.when(lax.axis_index("tensor") == q)
@@ -461,7 +470,7 @@
             source[rows, lanes] = key * conv_taps(padded, 2, place, taps_v, lanes)
         return carry
 
-    lax.fori_loop(0, CHUNKS, conv_step, 0)
+    lax.fori_loop(0, CHUNKS, conv_step, 0, unroll=2)
 
     tick(2)
 
@@ -505,6 +514,11 @@
                     mixed_own[:, low - q * width : high - q * width] = mixed[:, low - part * CT : high - part * CT]
 
     tick(4)
+
+    @pl.when(tile == D // CT - 1)
+    def _():
+        for copy in own_quarter():
+            copy.wait()
 
 
 def mixer_backward_kernel(
@@ -841,7 +855,7 @@
                     sums += [(held * each).reshape(CHUNK // 8, 8, 128).sum(0) for each in (now, one, two)]
                 return tuple(a + b for a, b in zip(carry, sums))
 
-            sums = lax.fori_loop(0, CHUNKS, second_step, tuple(jnp.zeros((8, 128), F32) for _ in range(9)))
+            sums = lax.fori_loop(0, CHUNKS, second_step, tuple(jnp.zeros((8, 128), F32) for _ in range(9)), unroll=2)
             for index, each in enumerate(sums):
                 row = MISC_TAPS + 16 * half + index
                 misc[tile, row : row + 1, :] = jnp.sum(each, axis=0, keepdims=True)
@@ -1295,19 +1309,20 @@
         return pltpu.make_async_copy(self.whole.at[origin], self.flush.at[origin], self.local_sems.at[1 + index])
 
     def gather_start(self):
-        self.own_copy().start()
         self.cross_start()
-        self.spread_start(0, 0)
+        if not self.relay:
+            self.own_copy().start()
+            self.spread_start(0, 0)
 
     def settle(self):
         if self.flush is not None:
-            for index in range(len(self.origins)):
+            for index in range(1 if self.relay else 0, len(self.origins)):
                 self.flush_copy(index).wait()
         for stream in range(2):
             if self.held is not None:
                 for k in range(self.bits):
                     self.sum_copy(stream, k).wait_send()
-            for index in range(len(self.origins)):
+            for index in range(1 if self.relay else 0, len(self.origins)):
                 for j in range(self.bits):
                     self.spread_all(stream, index, j).wait_send()
         if not self.relay:
@@ -1364,7 +1379,7 @@
         for index in range(len(self.origins)):
             if index:
                 put(ahead + (index - 1 if self.relay else 0), arrive, index)
-            for j in range(bits):
+            for j in range(bits if index or not self.relay else 0):
                 put(ahead + (index if self.relay else min(index, 1)) + j, advance, index, j)
         put(len(steps), self.settle)
         return steps
@@ -1482,7 +1497,7 @@
         normed[rows, :] = (held * gain + shift).astype(BF16)
         return carry
 
-    lax.fori_loop(0, count // PASS, norm_step, 0, unroll=3)
+    lax.fori_loop(0, count // PASS, norm_step, 0, unroll=9)
 
     for block in range(NB):
         window = normed[:, WBASE[block] : WBASE[block] + 256]
@@ -1516,7 +1531,7 @@
                 silu[out, rows, lanes] = joined(passed * mask)
             return inside
 
-        lax.fori_loop(0, count // PASS, ahead_rows, 0, unroll=3)
+        lax.fori_loop(0, count // PASS, ahead_rows, 0, unroll=9)
         return carry
 
     lax.fori_loop(0, width // 128, ahead_lanes, 0)
@@ -1561,7 +1576,7 @@
             grad_summed[block, rows, :] = total.reshape(16, 256).astype(BF16)
         return carry
 
-    lax.fori_loop(0, count // 16, down_step, 0, unroll=2)
+    lax.fori_loop(0, count // 16, down_step, 0, unroll=6)
 
     for block in range(NB):
         grad_inner[block] = dot_nt(grad_summed[block], down_weight[block])
@@ -1588,7 +1603,7 @@
                             sums[which + block * NB + out, :, lanes] += (held * terms[out]).sum(0)
             return inside
 
-        lax.fori_loop(0, count // PASS, run, 0, unroll=3)
+        lax.fori_loop(0, count // PASS, run, 0, unroll=9)
 
     kept = -(-own // 128)
     for tile in range(kept):
@@ -1626,7 +1641,7 @@
         branch[rows, :] = out.astype(BF16)
         return carry
 
-    lax.fori_loop(0, count // PASS, norm_back, 0, unroll=3)
+    lax.fori_loop(0, count // PASS, norm_back, 0, unroll=9)
 
     grad_mixed[...] = dot_nt(branch[...], out_weight[...]).astype(BF16)
     grad_out[0:own, :] += dot_tn(mixed_own[...], branch[...])
@@ -1756,7 +1771,8 @@
         + [whole_spec(features)],
         out_specs=out_specs,
         out_shape=outs,
-        scratch_shapes=vmem_specs(scratch) + Exchange.semaphores(ranks, quarters),
+        scratch_shapes=vmem_specs(scratch) + [pltpu.SemaphoreType.DMA((ranks,))]
+        + Exchange.semaphores(ranks, quarters),
         compiler_params=collective(0),
         cost_estimate=pl.CostEstimate(flops=12_000_000_000, bytes_accessed=40_000_000, transcendentals=2_000_000),
         name="mixer_forward",

time: 291 us -> 270 us (0.928)
  Pallas kernels: 290 us -> 269 us
    pallas_call x1, Pallas kernels: 74 us -> 64.9 us  [mixer_forward(): pl.pallas_call(kernel, grid=(D // CT,), in_specs=[pl.BlockSpec(memory_spa...]
    pallas_call x1, Pallas kernels: 69 us -> 61 us  [glu(): pl.pallas_call(glu_kernel, grid=(TOK // count,), in_specs=[tile(D), tile(...]
    pallas_call x1, Pallas kernels: 134 us -> 130 us  [mixer_backward(): pl.pallas_call(functools.partial(mixer_backward_kernel, ranks, quarters),...]
where the time goes in v1:
time: 270 us; the launch traced here: 269 us
  Pallas kernels  269 us (100%)
    pallas_call x1, Pallas kernels, mixer_backward(): pl.pallas_call(functools.partial(mixer_backward_kernel, ranks, quarters),...  130 us
    pallas_call x1, Pallas kernels, mixer_forward(): pl.pallas_call(kernel, grid=(D // CT,), in_specs=[pl.BlockSpec(memory_spa...  64.9 us
    pallas_call x1, Pallas kernels, glu(): pl.pallas_call(glu_kernel, grid=(TOK // count,), in_specs=[tile(D), tile(...  61 us
    pallas_call x1, Pallas kernels, unpack(): pl.pallas_call(functools.partial(unpack_kernel, quarters), in_specs=[any_...  13.1 us

profile of v1, /device:TPU:0, one launch (start us, length us, event | category | flops | bytes accessed | tf_op | source)
XLA Modules:
  0.0 269.4 jit_solution(18146328589331780478)
XLA Ops:
  0.7 64.9 %mixer_forward.1 = (bf16[1152,768]{1,0:T(8,128)(2,1)}, bf16[1152,768]{1,0:T(8,128)(2,1)}, bf16[1152,768]{1,0:T(8,128)(2,1)}, bf16[1152,768]{1,0:T(8,128)(2,1)}, ...) custom-call(s32[3]{0:T(128)} %refs_0_.1, ...), custom_call_target="tpu_custom_call" | custom-call | flops 12000000000 | bytes 40000000 | tf_op jit(solution)/shard_map/mixer_forward/pallas_call | solution.py:1765
  65.5 61.0 %glu.1 = (f32[1152,768]{1,0:T(8,128)}, f32[1152,768]{1,0:T(8,128)}, bf16[1152,768]{1,0:T(8,128)(2,1)}, f32[3584,128]{1,0:T(8,128)}, f32[192,768]{1,0:T(8,128)}) custom-call(bf16[1152,768]{1,0:T(8,128)(2,1)} %tokens.3, bf16[1152,768]{1,0:T(8,128)(2,1)} %cotangent.1, bf16[1152,768]{1,0:T(8,128)(2,1)} %get-tuple-element.69.mixed, ...), custom_call_target="tpu_custom_call" | custom-call | flops 14000000000 | bytes 40000000 | tf_op jit(solution)/shard_map/glu/pallas_call | solution.py:1914
  126.5 129.7 %mixer_backward.1 = (f32[1152,768]{1,0:T(8,128)}, f32[1,2,2,2,448,128]{5,4,3,2,1,0:T(8,128)}, f32[4,2,2,2,24,768]{5,4,3,2,1,0:T(8,128)}, f32[3,4,2,2,2,24,768]{6...) custom-call(f32[3584,128]{1,0:T(8,128)} %get-tuple-element.75.early, ...), custom_call_target="tpu_custom_call" | custom-call | flops 14000000000 | bytes 40000000 | tf_op jit(solution)/shard_map/mixer_backward/pallas_call | solution.py:1855
  256.2 13.1 %unpack.1 = (f32[1152,768]{1,0:T(8,128)}, f32[768,2304]{1,0:T(8,128)}, f32[768,768]{1,0:T(8,128)}, f32[128,1536]{1,0:T(8,128)}, f32[128,128]{1,0:T(8,128)}, /*in...) custom-call(f32[1152,768]{1,0:T(8,128)} %get-tuple-element.92.grad_t, ...), custom_call_target="tpu_custom_call" | custom-call | bytes 30000000 | tf_op jit(solution)/shard_map/unpack/pallas_call | solution.py:2065

commit v2 on v1

--- a/solution.py
+++ b/solution.py
@@ -736,19 +736,20 @@
     total = tiles * (front + back)
     due = [[] for _ in range(total)]
     late = []
+    spots = [spot for spot in range(total) if spot < tiles * front + back or (spot - tiles * front) % back > 3]
 
     def plan(levels, start, pace, stop):
         for level, events in enumerate(levels):
-            if stop is None and start + pace * level >= total:
+            if stop is None and start + pace * level >= len(spots):
                 late.append(events)
             else:
-                due[min(start + pace * level, (total if stop is None else stop) - 1)] += events
-
-    plan(early_exchange.levels(), 3, 4, total)
+                due[spots[min(start + pace * level, (len(spots) if stop is None else stop) - 1)]] += events
+
+    plan(early_exchange.levels(), 3, 5, len(spots))
     plan(out_exchange.levels(), 2, 3, tiles * front - 1)
     for job in range(tiles):
-        plan(tile_exchange(job, (job + 1) % 3).levels(), (job + 1) * front + 1, 3 if job < last else 2, total)
-    plan(other_exchange.levels(), total - back + 4, 1, None)
+        plan(tile_exchange(job, (job + 1) % 3).levels(), (job + 1) * front + 1, (4, 3, 2)[job], len(spots))
+    plan(other_exchange.levels(), len(spots) - 5, 1, None)
 
     def tick(base, phase, width):
         for index in range(tiles):

time: 270 us -> 263 us (0.974)
  Pallas kernels: 269 us -> 261 us
    pallas_call x1, Pallas kernels: 130 us -> 123 us  [mixer_backward(): pl.pallas_call(functools.partial(mixer_backward_kernel, ranks, quarters),...]
where the time goes in v2:
time: 263 us; the launch traced here: 262 us
  Pallas kernels  261 us (99%)
    pallas_call x1, Pallas kernels, mixer_backward(): pl.pallas_call(functools.partial(mixer_backward_kernel, ranks, quarters),...  123 us
    pallas_call x1, Pallas kernels, mixer_forward(): pl.pallas_call(kernel, grid=(D // CT,), in_specs=[pl.BlockSpec(memory_spa...  64.9 us
    pallas_call x1, Pallas kernels, glu(): pl.pallas_call(glu_kernel, grid=(TOK // count,), in_specs=[tile(D), tile(...  61 us
    pallas_call x1, Pallas kernels, unpack(): pl.pallas_call(functools.partial(unpack_kernel, quarters), in_specs=[any_...  13.1 us

profile of v2, /device:TPU:0, one launch (start us, length us, event | category | flops | bytes accessed | tf_op | source)
XLA Modules:
  0.0 262.3 jit_solution(8929343314045911312)
XLA Ops:
  0.7 64.9 %mixer_forward.1 = (bf16[1152,768]{1,0:T(8,128)(2,1)}, bf16[1152,768]{1,0:T(8,128)(2,1)}, bf16[1152,768]{1,0:T(8,128)(2,1)}, bf16[1152,768]{1,0:T(8,128)(2,1)}, ...) custom-call(s32[3]{0:T(128)} %refs_0_.1, ...), custom_call_target="tpu_custom_call" | custom-call | flops 12000000000 | bytes 40000000 | tf_op jit(solution)/shard_map/mixer_forward/pallas_call | solution.py:1766
  65.5 61.0 %glu.1 = (f32[1152,768]{1,0:T(8,128)}, f32[1152,768]{1,0:T(8,128)}, bf16[1152,768]{1,0:T(8,128)(2,1)}, f32[3584,128]{1,0:T(8,128)}, f32[192,768]{1,0:T(8,128)}) custom-call(bf16[1152,768]{1,0:T(8,128)(2,1)} %tokens.3, bf16[1152,768]{1,0:T(8,128)(2,1)} %cotangent.1, bf16[1152,768]{1,0:T(8,128)(2,1)} %get-tuple-element.69.mixed, ...), custom_call_target="tpu_custom_call" | custom-call | flops 14000000000 | bytes 40000000 | tf_op jit(solution)/shard_map/glu/pallas_call | solution.py:1915
  126.5 122.6 %mixer_backward.1 = (f32[1152,768]{1,0:T(8,128)}, f32[1,2,2,2,448,128]{5,4,3,2,1,0:T(8,128)}, f32[4,2,2,2,24,768]{5,4,3,2,1,0:T(8,128)}, f32[3,4,2,2,2,24,768]{6...) custom-call(f32[3584,128]{1,0:T(8,128)} %get-tuple-element.75.early, ...), custom_call_target="tpu_custom_call" | custom-call | flops 14000000000 | bytes 40000000 | tf_op jit(solution)/shard_map/mixer_backward/pallas_call | solution.py:1856
  249.1 13.1 %unpack.1 = (f32[1152,768]{1,0:T(8,128)}, f32[768,2304]{1,0:T(8,128)}, f32[768,768]{1,0:T(8,128)}, f32[128,1536]{1,0:T(8,128)}, f32[128,128]{1,0:T(8,128)}, /*in...) custom-call(f32[1152,768]{1,0:T(8,128)} %get-tuple-element.92.grad_t, ...), custom_call_target="tpu_custom_call" | custom-call | bytes 30000000 | tf_op jit(solution)/shard_map/unpack/pallas_call | solution.py:2066
